TPU v7x, 32 devices: a whole 2x2x4 slice. The times are simulated.
32 devices in a mesh: dp: 8 (over z, y), tensor: 4 (over x, core).
Axes of the slice: x: 2, y: 2, z: 4, core: 2. Of those that a mesh axis runs over, the one named last changes fastest.
Arguments:
- block_input: bfloat16 [7680, 1536], P('dp'), may hold values from -6 to 6
- norm1_gain: float32 [1536], replicated, may hold values from 0.1 to 1.9
- query_weight: bfloat16 [1536, 1536], P(None, 'tensor'), may hold values from -0.15625 to 0.15625
- keyvalue_weight: bfloat16 [1536, 256], replicated, may hold values from -0.15625 to 0.15625
- out_weight: bfloat16 [1536, 1536], P('tensor'), may hold values from -0.625 to 0.625
- norm2_gain: float32 [1536], replicated, may hold values from 0.1 to 1.9
- gate_up_weight: bfloat16 [2, 1536, 4608], P(None, None, 'tensor'), may hold values from -0.15625 to 0.15625
- down_weight: bfloat16 [4608, 1536], P('tensor'), may hold values from -0.1875 to 0.1875
- cotangent: bfloat16 [7680, 1536], P('dp'), may hold values from -6 to 6
Outputs:
- block_output: bfloat16 [7680, 1536], P('dp')
- input_grad: bfloat16 [7680, 1536], P('dp')
- norm1_grad: float32 [1536], replicated
- query_grad: float32 [1536, 1536], P(None, 'tensor')
- keyvalue_grad: float32 [1536, 256], replicated
- out_grad: float32 [1536, 1536], P('tensor')
- norm2_grad: float32 [1536], replicated
- gate_up_grad: float32 [2, 1536, 4608], P(None, None, 'tensor')
- down_grad: float32 [4608, 1536], P('tensor')
All inputs are finite; a program needn't handle non-finite values.
Results may differ from a plain program's by a relative error of at most 0.025.
Values may be sent and summed in bfloat16 or wider, within the bound.
No kernel may reach another device: no remote copies, remote signals or barrier semaphores. Data moves between devices by JAX's collectives and lax.ppermute only.
A program may use at most 192 MiB of HBM per device.

v0:
```python
import functools
import math

import jax
import jax.numpy as jnp
import numpy as np
from jax import lax
from jax.experimental import pallas as pl
from jax.experimental.pallas import tpu as pltpu
from jax.sharding import PartitionSpec as P

WINDOW = 1024
EPSILON = 1e-06
GELU_COEF = 0.7978845608028654
BF16 = jnp.bfloat16
F32 = jnp.float32
NN = (((1,), (0,)), ((), ()))
NT = (((1,), (1,)), ((), ()))
TN = (((0,), (0,)), ((), ()))

RING = (0, 2, 4, 6, 7, 5, 3, 1)

ANY = pl.BlockSpec(memory_space=pl.ANY)
SMEM = pl.BlockSpec(memory_space=pltpu.SMEM)
VMEM = pl.BlockSpec(memory_space=pltpu.VMEM)
MIB = 2**20
COST = pl.CostEstimate(flops=0, bytes_accessed=0, transcendentals=0)

ORDER = " ".join(
    (
        "project attend0 attend1 dhidden0",
        "norm0 dhidden1 ffn0 dnsib0",
        "norm1 ffn1 wide dnown0",
        "down b a dnsib1",
        "a dnown1 b a",
        "nback0 a aback0 nback1",
        "b a aback1 a",
        "b late kv a",
        "b fosib1 fosib0 kvpart",
        "a dn11 E b",
        "e e b a",
        "e input1 dn10 foown0",
        "e a b e",
        "input0 sums e a",
        "b sums1 sums2 e",
        "foown1 sums4 e b",
        "out0 e sumscore a",
        "e out1 sumschip b",
        "e weave a b",
        "a e sumsend putdown",
        "e b putwide0 e",
        "putlate b putwide1",
    )
).split()


def dot(left, right, dims=NN):
    return lax.dot_general(left, right, dims, preferred_element_type=F32)


def swap_core(field):
    return lax.ppermute(field, "tensor", [(i, i ^ 1) for i in range(4)])


def swap_x(field):
    return lax.ppermute(field, "tensor", [(i, i ^ 2) for i in range(4)])


def shape(dims, dtype):
    return jax.ShapeDtypeStruct(dims, dtype)


def whole(array):
    rank = len(array.shape)
    return pl.BlockSpec(array.shape, lambda *_: (0,) * rank)


class Chain:
    def __init__(self):
        self.token = None

    def call(self, body, outs, ins, in_specs, out_specs, grid=(1,), scalars=(), vmem=16, scratch=(), aliases=None, far=(),
        far_ins=(), near=(),
    ):
        tokens = [] if self.token is None else [self.token]
        given, made = len(scalars) + len(ins), len(outs)

        def run(*refs):
            refs = refs[:given] + refs[given + len(tokens) :]
            body(*refs[: given + made], *refs[given + made + 1 :])

        outs = [pltpu.HBM(o.shape, o.dtype) if i in far else o for i, o in enumerate(outs)]
        outs = [pltpu.VMEM(o.shape, o.dtype) if i in near else o for i, o in enumerate(outs)]
        ins = [pltpu.with_memory_space_constraint(a, pltpu.HBM) if i in far_ins else a for i, a in enumerate(ins)]
        *results, self.token = pl.pallas_call(
            run,
            out_shape=outs + [shape((8, 128), F32)],
            grid_spec=pltpu.PrefetchScalarGridSpec(
                num_scalar_prefetch=len(scalars),
                grid=grid,
                in_specs=list(in_specs) + [ANY] * len(tokens),
                out_specs=list(out_specs) + [ANY],
                scratch_shapes=list(scratch),
            ),
            input_output_aliases=aliases or {},
            compiler_params=pltpu.CompilerParams(vmem_limit_bytes=vmem * MIB),
            cost_estimate=COST,
        )(*scalars, *ins, *tokens)
        return results

    def direct(self, body, outs, ins, scalars=(), far_ins=(), far=(), vmem=16, scratch=()):
        tokens = [] if self.token is None else [self.token]
        given, made = len(scalars) + len(ins), len(outs)

        def run(*refs):
            refs = refs[:given] + refs[given + len(tokens) :]
            body(*refs[: given + made], *refs[given + made + 1 :])

        ins = [pltpu.with_memory_space_constraint(a, pltpu.HBM) if i in far_ins else a for i, a in enumerate(ins)]
        in_specs = [SMEM] * len(scalars) + [ANY if i in far_ins else VMEM for i in range(len(ins))]
        *results, self.token = pl.pallas_call(
            run,
            out_shape=[pltpu.HBM(o.shape, o.dtype) if i in far else o for i, o in enumerate(outs)]
            + [shape((8, 128), F32)],
            in_specs=in_specs + [ANY] * len(tokens),
            out_specs=[ANY if i in far else VMEM for i in range(made)] + [ANY],
            scratch_shapes=list(scratch),
            compiler_params=pltpu.CompilerParams(vmem_limit_bytes=vmem * MIB),
            cost_estimate=COST,
        )(*scalars, *ins, *tokens)
        return results

    def after(self, *values):
        *values, self.token = lax.optimization_barrier((*values, self.token))
        return values


def rope(field, table, sign=1.0):
    half = field.shape[1] // 2
    other = pltpu.roll(table, half, 1)
    first = lax.broadcasted_iota(jnp.int32, table.shape, 1) < half
    cosine = jnp.where(first, table, other)
    sine = jnp.where(first, -other, table) * sign
    return field * cosine + pltpu.roll(field, half, 1) * sine


def rms_factor(field):
    return lax.rsqrt(jnp.mean(field * field, axis=1, keepdims=True) + EPSILON)


def start_all(sources, targets, done, first=0):
    copies = [pltpu.make_async_copy(s, t, done.at[first + i]) for i, (s, t) in enumerate(zip(sources, targets))]
    for copy in copies:
        copy.start()
    return copies


def project_kernel(
    core, gain, x, weight, table, keys, values, own0, own1, table0, table1, x_rows, weight_all, table_all, done
):
    quarter = own0.shape[0]
    head_dim = keys.shape[1]

    def rows(block):
        return pl.ds(block * quarter, quarter)

    copies = start_all([x.at[rows(i)] for i in range(4)], [x_rows.at[rows(i)] for i in range(4)], done)
    copies += start_all((weight, table), (weight_all, table_all), done, 4)
    for block in range(4):
        here = rows(block)
        copies[block].wait()
        field = x_rows[here, :].astype(F32)
        normed = (field * rms_factor(field) * gain[...]).astype(BF16)
        if block == 0:
            copies[4].wait()
            copies[5].wait()
        both = dot(normed, weight_all[...])
        keys[here, :] = rope(both[:, :head_dim], table_all[here, :]).astype(BF16)
        values[here, :] = both[:, head_dim:].astype(BF16)
        number, own, angles = (core[0], own0, table0) if block < 2 else (3 - core[0], own1, table1)

        @pl.when(number == block)
        def _():
            own[...] = normed
            angles[...] = table_all[here, :]


def causal(rows, columns, first_row):
    row = lax.broadcasted_iota(jnp.int32, (rows, columns), 0) + first_row
    column = lax.broadcasted_iota(jnp.int32, (rows, columns), 1)
    allowed = column <= row
    if columns > WINDOW:
        allowed = allowed & (row - column < WINDOW)
    return allowed


def attend(numbers, scale, block, normed, keys, values, table, query_w, out_w, part, rot_q, head_out, log_total, arriving):
    quarter = normed.shape[0]
    head_dim = keys.shape[1]
    heads = out_w.shape[0] // head_dim
    for side in range(2):
        arriving[side].wait()
        queries = dot(normed[...], query_w[side])
        for head in range(heads // 2):
            columns = slice(head * head_dim, (head + 1) * head_dim)
            place = side * (heads // 2) + head
            rot_q[:, place * head_dim : (place + 1) * head_dim] = (
                rope(queries[:, columns], table[...]) * scale
            ).astype(BF16)
    for number in numbers:

        @pl.when(block[0] == number)
        def _():
            span = (number + 1) * quarter
            allowed = causal(quarter, span, number * quarter)
            lane = lax.broadcasted_iota(jnp.int32, log_total.shape, 1)

            def two_heads(pair, _):
                for head in (2 * pair, 2 * pair + 1):
                    columns = pl.ds(pl.multiple_of(head * head_dim, head_dim), head_dim)
                    scores = dot(rot_q[:, columns], keys[:span, :], NT)
                    scores = jnp.where(allowed, scores, -1e30)
                    top = jnp.max(scores, axis=1, keepdims=True)
                    weights = jnp.exp(scores - top)
                    total = jnp.sum(weights, axis=1, keepdims=True)
                    probs = (weights * (1.0 / total)).astype(BF16)
                    head_out[:, columns] = dot(probs, values[:span, :]).astype(BF16)
                    log_total[...] = jnp.where(lane == head, top + jnp.log(total), log_total[...])
                return 0

            lax.fori_loop(0, heads // 2, two_heads, 0)

    arriving[2].wait()
    arriving[3].wait()
    part[...] = dot(head_out[...], out_w[...]).astype(BF16)


def attend_kernel(
    numbers, scale, gather, block, places, normed, keys, values, table, query_own, query_sib, out_own, out_sib, *refs
):
    *refs, query_w, out_w, done = refs
    columns = out_own.shape[0]
    weights = start_all(
        (query_own, query_sib, out_own, out_sib),
        (query_w.at[0], query_w.at[1], out_w.at[pl.ds(0, columns)], out_w.at[pl.ds(columns, columns)]),
        done,
    )
    if gather:
        cotangent, gate_up, part, rot_q, head_out, log_total, far_normed, far_keys, far_values, cot0, cot1, near_gate_up = refs
        quarter = normed.shape[0]
        rows = [cotangent.at[pl.ds(pl.multiple_of(places[i] * quarter, 16), quarter)] for i in range(4)]
        halves = [cot.at[pl.ds(i * quarter, quarter)] for cot in (cot0, cot1) for i in range(2)]
        sources, targets = (keys, values, *rows, gate_up), (far_keys, far_values, *halves, near_gate_up)
    else:
        down, part, rot_q, head_out, log_total, far_normed, near_down = refs
        sources, targets = (down,), (near_down,)
    kept = start_all((normed, *sources), (far_normed, *targets), done, 4)
    attend(numbers, scale, block, normed, keys, values, table, query_w, out_w, part, rot_q, head_out, log_total, weights)
    for copy in kept:
        copy.wait()


def attend_back_kernel(scale, order, core, rot_q, log_total, d_heads, keys, values, table, *refs):
    if order == 0:
        d_queries, wide_keys, wide_values = refs
        wide_keys[...] = jnp.zeros_like(wide_keys)
        wide_values[...] = jnp.zeros_like(wide_values)
    else:
        before_keys, before_values, d_queries, kv_own, kv_sib, d_keys, d_values, wide_keys, wide_values = refs
        wide_keys[...] = before_keys[...]
        wide_values[...] = before_values[...]
    quarter = rot_q.shape[0]
    head_dim = keys.shape[1]
    block = core[0] if order == 0 else 3 - core[0]
    for number in (0, 1) if order == 0 else (2, 3):

        @pl.when(block == number)
        def _():
            span = (number + 1) * quarter
            own_table = table[number * quarter : span, :]
            allowed = causal(quarter, span, number * quarter)
            for head in range(rot_q.shape[1] // head_dim):
                columns = slice(head * head_dim, (head + 1) * head_dim)
                query = rot_q[:, columns]
                d_out = d_heads[:, columns]
                scores = dot(query, keys[:span, :], NT) - log_total[:, head : head + 1]
                probs = jnp.exp(jnp.where(allowed, scores, -1e30))
                d_probs = dot(d_out, values[:span, :], NT)
                delta = jnp.sum(probs * d_probs, axis=1, keepdims=True)
                d_scores = (probs * (d_probs - delta)).astype(BF16)
                d_query = dot(d_scores, keys[:span, :]) * scale
                d_queries[:, columns] = rope(d_query, own_table, -1.0).astype(BF16)
                wide_keys[:, :span] += dot(query, d_scores, TN)
                wide_values[:, :span] += dot(d_out, probs.astype(BF16), TN)

    if order == 0:
        return

    def rows_of(number):
        return pl.ds(pl.multiple_of(number * quarter, 16), quarter)

    d_keys[...] = rope(wide_keys[...].T, table[...], -1.0)
    d_values[...] = wide_values[...].T
    for place in range(2):
        rows = slice(place * quarter, (place + 1) * quarter)
        own = rows_of(core[0] if place == 0 else 3 - core[0])
        sib = rows_of(1 - core[0] if place == 0 else 2 + core[0])
        kv_own[rows, :head_dim] = d_keys[own, :]
        kv_own[rows, head_dim:] = d_values[own, :]
        kv_sib[rows, :head_dim] = d_keys[sib, :].astype(BF16)
        kv_sib[rows, head_dim:] = d_values[sib, :].astype(BF16)


def d_hidden_kernel(cotangent, weight, d_hidden):
    d_hidden[...] = dot(cotangent[...], weight[...], NT).astype(BF16)


def norm_kernel(block, x, part, from_x, gain, upper, lower, residual, x_rows, done):
    quarter = part.shape[0]
    here = x.at[pl.ds(pl.multiple_of(block[0] * quarter, 16), quarter)]
    (copy,) = start_all((here,), (x_rows,), done)
    total = part[...].astype(F32) + from_x[...].astype(F32)
    copy.wait()
    value = x_rows[...].astype(F32) + total
    residual[...] = value
    normed = (value * rms_factor(value) * gain[...]).astype(BF16)
    cut = upper.shape[0]
    upper[...] = normed[:cut, :]
    lower[...] = normed[cut:, :]


def ffn_kernel(own0, own1, sib0, sib1, weight, d_hidden, hidden, d_gate, d_up, normed):
    first = 0
    for rows in (own0, own1, sib0, sib1):
        normed[first : first + rows.shape[0], :] = rows[...]
        first += rows.shape[0]
    gate = dot(normed[...], weight[0])
    up = dot(normed[...], weight[1])
    square = gate * gate
    inner = jnp.tanh(GELU_COEF * gate * (1.0 + 0.044715 * square))
    bell = 0.5 * (1.0 + inner)
    gelu = gate * bell
    slope = bell + 0.5 * gate * (1.0 - inner * inner) * (GELU_COEF * (1.0 + 3.0 * 0.044715 * square))
    change = d_hidden[...].astype(F32)
    hidden[...] = (gelu * up).astype(BF16)
    d_gate[...] = (change * up * slope).astype(BF16)
    d_up[...] = (change * gelu).astype(BF16)


def down_grad_kernel(place, left0, left1, right0, right1, out):
    rows, tile = out.shape[1], out.shape[2] // 2
    for i in range(2):
        here = slice(i * tile, (i + 1) * tile)
        total = dot(left0[...], right0[:, here], TN) + dot(left1[...], right1[:, here], TN)
        for number in range(8):
            out[turned(place, number), :, here] = total[number * rows : (number + 1) * rows, :].astype(BF16)


def turned(places, number, side=0):
    return (places[side] - number) & 7


def wide_grad_kernel(tiles, place, left0, left1, gate0, gate1, up0, up1, out):
    rows, columns, chunks = out.shape[1], gate0.shape[1], 8 // tiles
    for side, (right0, right1) in enumerate(((gate0, gate1), (up0, up1))):
        for i in range(tiles):
            here = slice(i * chunks * rows, (i + 1) * chunks * rows)
            total = dot(left0[:, here], right0[...], TN) + dot(left1[:, here], right1[...], TN)
            for chunk in range(chunks):
                part = total[chunk * rows : (chunk + 1) * rows, :].astype(BF16)
                out[turned(place, i * chunks + chunk), :, side * columns : (side + 1) * columns] = part


def rows_kernel(side, tiles, dims, count, *refs):
    refs, joined = refs[:-count], refs[-count:]
    chunks = joined[0].shape[0] * 2 // refs[0].shape[0]
    lefts, weight = refs[: chunks * count], refs[chunks * count]
    *extra, out = refs[chunks * count + 1 :]
    quarter = out.shape[0] // chunks
    own = slice(side * quarter, (side + 1) * quarter)
    for i, target in enumerate(joined):
        for chunk in range(chunks):
            target[chunk * quarter : (chunk + 1) * quarter, :] = lefts[chunks * i + chunk][own, :]
    tile = out.shape[1] // tiles
    for t in range(tiles):
        here = slice(t * tile, (t + 1) * tile)
        total = None
        for i, left in enumerate(joined):
            right = weight[:, here] if dims == NN else weight[i, here, :]
            term = dot(left[...], right, dims)
            total = term if total is None else total + term
        if extra:
            total = total + extra[0][:, here].astype(F32)
        out[:, here] = total.astype(BF16)


def d_normed1_kernel(d_queries, own, sibling, out):
    half = own.shape[1]
    out[...] = (dot(d_queries[:, :half], own[...], NT) + dot(d_queries[:, half:], sibling[...], NT)).astype(BF16)


def norm_back(field, gain, d_normed):
    factor = rms_factor(field)
    scaled = gain * d_normed
    d_gain = jnp.sum(d_normed * field * factor, axis=0, keepdims=True)
    return factor * scaled - field * (factor * factor * factor) * jnp.mean(scaled * field, axis=1, keepdims=True), d_gain


def norm2_back_kernel(
    residual, on_chip, from_x, cotangent, gain, out_own, out_sib, d_residual, d_res_low, d_heads, d_gain
):
    d_normed = on_chip[...].astype(F32) + from_x[...].astype(F32)
    change, d_gain[...] = norm_back(residual[...], gain[...], d_normed)
    total = cotangent[...].astype(F32) + change
    d_residual[...] = total
    low = total.astype(BF16)
    d_res_low[...] = low
    half = out_own.shape[0]
    d_heads[:, :half] = dot(low, out_own[...], NT).astype(BF16)
    d_heads[:, half:] = dot(low, out_sib[...], NT).astype(BF16)


def norm1_back_kernel(block, x, on_chip, from_x, d_kv, d_residual, kv_weight, gain, d_input, d_gain):
    d_normed = (on_chip[...].astype(F32) + from_x[...].astype(F32)) + dot(d_kv[...], kv_weight[...], NT)
    change, d_gain[...] = norm_back(x[...].astype(F32), gain[...], d_normed)
    d_input[...] = (d_residual[...] + change).astype(BF16)


def late_grad_kernel(
    columns, place, normed0, normed1, d_queries0, d_queries1, head_out0, head_out1, d_res_low0, d_res_low1, mine, other
):
    rows = mine.shape[1]
    for side, out in enumerate((mine, other)):
        part = slice(side * columns, (side + 1) * columns)
        query = dot(normed0[...], d_queries0[:, part], TN) + dot(normed1[...], d_queries1[:, part], TN)
        outer = dot(head_out0[:, part], d_res_low0[...], TN) + dot(head_out1[:, part], d_res_low1[...], TN)
        folds = outer.shape[1] // columns
        short = rows // folds
        for number in range(8):
            spot = turned(place, number, side)
            out[spot, :, :columns] = query[number * rows : (number + 1) * rows, :].astype(out.dtype)
            for fold in range(folds):
                out[spot, fold * short : (fold + 1) * short, columns:] = outer[
                    number * short : (number + 1) * short, fold * columns : (fold + 1) * columns
                ].astype(out.dtype)


def weave_kernel(places, *refs):
    *refs, first, second, done = refs
    quarter = refs[0].shape[0]
    copies = []
    for i, source in enumerate(refs):
        target = (first, second)[i // 4]
        rows = pl.ds(pl.multiple_of(places[i % 4] * quarter, 16), quarter)
        copies += start_all((source,), (target.at[rows],), done, i)
    for copy in copies:
        copy.wait()


def assemble_kernel(first, old, count, place, *refs):
    pieces, refs = refs[:count], refs[count + old :]
    *targets, stage, done = refs
    rows, width = pieces[0].shape
    flying = [None, None]
    for i, piece in enumerate(pieces):
        slot = i % 2
        k = (place[0] - first - i) & 7
        for copy in flying[slot] or ():
            copy.wait()
        stage[slot] = piece[...].astype(F32)
        if len(targets) == 1 and targets[0].shape[0] == 2:
            half = width // 2
            moves = [(stage.at[slot, :, n * half : (n + 1) * half], targets[0].at[n, k]) for n in range(2)]
        elif len(targets) == 1:
            moves = [(stage.at[slot], targets[0].at[k])]
        else:
            half = width // 2
            folds = targets[1].shape[2] // half
            short = rows // folds
            moves = [(stage.at[slot, :, :half], targets[0].at[k])]
            moves += [
                (stage.at[slot, n * short : (n + 1) * short, half:], targets[1].at[k, :, n * half : (n + 1) * half])
                for n in range(folds)
            ]
        flying[slot] = [pltpu.make_async_copy(s, t, done.at[slot, n]) for n, (s, t) in enumerate(moves)]
        for copy in flying[slot]:
            copy.start()
    for copies in flying:
        for copy in copies or ():
            copy.wait()


def ring_orders():
    return [RING if tensor % 2 == 0 else RING[::-1] for tensor in range(4)]


def ring_pairs():
    return [
        (order[i] * 4 + tensor, order[(i + 1) % 8] * 4 + tensor) for tensor, order in enumerate(ring_orders()) for i in range(8)
    ]


class Ring:
    def __init__(self, chain, place):
        self.chain, self.place, self.left = chain, place, 0

    def begin(self, field):
        self.field, self.travelling, self.pieces, self.left = field, field[1], [], 14
        self.send()

    def send(self):
        self.arrived = lax.ppermute(self.travelling, ("dp", "tensor"), ring_pairs())

    def step(self):
        if self.left == 0:
            raise ValueError("ring idle")
        self.left -= 1
        number = 14 - self.left
        (self.travelling,) = self.chain.after(self.arrived)
        if number <= 7:
            mine = self.field[(number + 1) % 8].astype(F32)
            (self.travelling,) = self.chain.after((self.travelling.astype(F32) + mine).astype(BF16))
        if number >= 7:
            self.pieces.append(self.travelling)
        if self.left:
            self.send()

    def assemble(self, targets, first, last):
        pieces = self.pieces[first:last]
        old = [t for t in targets if isinstance(t, jax.Array)]
        return self.chain.call(
            functools.partial(assemble_kernel, first, len(old), len(pieces)),
            [shape(t.shape, F32) for t in targets],
            [*pieces, *old],
            [whole(p) for p in pieces] + [ANY] * len(old),
            [ANY] * len(targets),
            scalars=[self.place],
            scratch=[pltpu.VMEM((2,) + pieces[0].shape, F32), pltpu.SemaphoreType.DMA((2, 8))],
            aliases={1 + len(pieces) + i: i for i in range(len(old))},
            vmem=16,
        )


class Whole:
    def __init__(self, chain, place):
        self.chain, self.place = chain, place

    def begin(self, field):
        total = lax.psum(field, "dp")
        self.pieces = [total[i] for i in range(8)]

    def step(self):
        pass

    assemble = Ring.assemble


def over_dp(field, step, n_dp):
    return field.astype(F32) + lax.ppermute(field, "dp", [(i, i ^ step) for i in range(n_dp)]).astype(F32)


class Block:
    def __init__(self, n_dp, args):
        (
            self.x, self.gain1, self.query_w, self.kv_w, self.out_w, self.gain2, self.gate_up_w, self.down_w, self.cot_in,
        ) = args
        self.gain1, self.gain2 = self.gain1[None], self.gain2[None]
        self.n_dp = n_dp
        self.length, self.width = self.x.shape
        self.quarter, self.half = self.length // 4, self.length // 2
        self.head_dim = self.kv_w.shape[1] // 2
        self.cols = self.query_w.shape[1]
        self.units = self.down_w.shape[0]
        self.middle = self.width // 2
        self.scale = 1.0 / math.sqrt(self.head_dim)
        tensor = lax.axis_index("tensor")
        self.core, self.chip = tensor & 1, tensor >> 1
        core = self.core
        self.own = jnp.stack([core, 3 - core])
        self.places = jnp.stack([core, 1 - core, 3 - core, 2 + core])
        self.weave_places = jnp.stack([core, 3 - core, 1 - core, 2 + core])
        self.chain = Chain()
        if n_dp == 8:
            dp = lax.axis_index("dp")
            z, y = dp >> 1, dp & 1
            forward = z + y * (7 - 2 * z)
            place = forward + core * (7 - 2 * forward)
            self.ring_place = jnp.stack([place, 7 - place])
        else:
            self.ring_place = jnp.zeros(2, jnp.int32)
        ring = Ring if n_dp == 8 else Whole
        self.ring_a, self.ring_b, self.ring_e = (ring(self.chain, self.ring_place) for _ in range(3))
        half_dim = self.head_dim // 2
        angle = np.arange(self.length)[:, None] * 10000.0 ** (-2.0 * np.arange(half_dim)[None, :] / self.head_dim)
        self.table = jnp.asarray(np.concatenate([np.cos(angle), np.sin(angle)], 1), F32)
        self.query_sib = swap_core(self.query_w)
        self.out_sib = swap_core(self.out_w)
    def rows(self, table=None):
        if table is None:
            return pl.BlockSpec((self.quarter, self.width), lambda i, *_: (i, 0))
        return pl.BlockSpec((self.quarter, self.width), lambda i, places: (places[i], 0))

    def project(self):
        q, d, w, n = self.quarter, self.head_dim, self.width, self.length
        outs = [shape((n, d), BF16)] * 2 + [shape((q, w), BF16)] * 2 + [shape((q, d), F32)] * 2
        self.keys, self.values, own0, own1, table0, table1 = self.chain.direct(
            project_kernel,
            outs,
            [self.gain1, self.x, self.kv_w, self.table],
            scalars=[self.core[None]],
            far_ins=(1, 2, 3),
            scratch=[
                pltpu.VMEM(self.x.shape, BF16), pltpu.VMEM(self.kv_w.shape, BF16), pltpu.VMEM(self.table.shape, F32),
                pltpu.SemaphoreType.DMA((6,)),
            ],
        )
        self.normed1, self.own_tables, self.far_normed1 = (own0, own1), (table0, table1), []

    def attend(self, j):
        q, w, c = self.quarter, self.width, 2 * self.cols
        ins = [
            self.normed1[j], self.keys, self.values, self.own_tables[j],
            self.query_w, self.query_sib, self.out_w, self.out_sib,
        ]
        blocks = [shape((q, w), BF16), shape((q, c), BF16), shape((q, c), BF16), shape((q, 8), F32)]
        outs = [shape((q, w), BF16)]
        if j == 1:
            more, narrow, rows = [self.cot_in, self.gate_up_w], shape(self.keys.shape, BF16), shape((self.half, w), BF16)
            outs += [narrow, narrow, rows, rows, shape(self.gate_up_w.shape, BF16)]
        else:
            more = [self.down_w]
            outs += [shape(self.down_w.shape, BF16)]
        part, rot_q, head_out, log_total, far_normed, *rest = self.chain.call(
            functools.partial(attend_kernel, (0, 1) if j == 0 else (2, 3), self.scale, j == 1),
            blocks + outs,
            ins + more,
            [whole(a) for a in ins[:4]] + [ANY] * (4 + len(more)),
            [whole(b) for b in blocks] + [ANY] * len(outs),
            scalars=[self.own[j : j + 1], self.places],
            scratch=[
                pltpu.VMEM((2,) + self.query_w.shape, BF16),
                pltpu.VMEM((c, w), BF16),
                pltpu.SemaphoreType.DMA((12,)),
            ],
            far=range(1, 7) if j == 1 else range(1, 5),
            near=range(7, 10) if j == 1 else (5,),
            far_ins=range(4, 10),
            vmem=20,
        )
        self.far_normed1.append(far_normed)
        return part, rot_q, head_out, log_total, rest

    def attend0(self):
        self.part0, self.rot_q0, self.head_out0, self.log0, (self.near_down,) = self.attend(0)
        self.from_x0 = swap_x(self.part0)

    def attend1(self):
        self.part1, self.rot_q1, self.head_out1, self.log1, rest = self.attend(1)
        self.far_keys, self.far_values, cot0, cot1, self.near_gate_up = rest
        self.cot = (cot0, cot1)
        self.from_x1 = swap_x(self.part1)

    def dhidden(self, j):
        return self.chain.direct(
            d_hidden_kernel, [shape((self.half, self.units), BF16)], [self.cot[j], self.near_down]
        )[0]

    def dhidden0(self):
        self.d_hidden0 = self.dhidden(0)

    def dhidden1(self):
        self.d_hidden1 = self.dhidden(1)

    def norm(self, j, part, from_x):
        upper = (self.quarter // 32 + 1) * 16
        outs = [shape((rows, self.width), BF16) for rows in (upper, self.quarter - upper)]
        outs.append(shape((self.quarter, self.width), F32))
        upper, lower, residual = self.chain.direct(
            norm_kernel,
            outs,
            [self.x, part, from_x, self.gain2],
            scalars=[self.own[j : j + 1]],
            far_ins=(0,),
            scratch=[pltpu.VMEM((self.quarter, self.width), BF16), pltpu.SemaphoreType.DMA((1,))],
        )
        return [upper, lower, swap_core(upper), swap_core(lower)], residual

    def norm0(self):
        self.normed2_0, self.residual0 = self.norm(0, self.part0, self.from_x0)

    def norm1(self):
        self.normed2_1, self.residual1 = self.norm(1, self.part1, self.from_x1)

    def ffn(self, normed, d_hidden):
        return self.chain.direct(
            ffn_kernel,
            [shape((self.half, self.units), BF16)] * 3 + [shape((self.half, self.width), BF16)],
            [*normed, self.near_gate_up, d_hidden],
        )

    def ffn0(self):
        self.wide0 = self.ffn(self.normed2_0, self.d_hidden0)

    def ffn1(self):
        self.wide1 = self.ffn(self.normed2_1, self.d_hidden1)
        self.hidden, self.d_gate, self.d_up, self.normed2 = zip(self.wide0, self.wide1)

    def down(self):
        (grad,) = self.chain.direct(
            down_grad_kernel,
            [shape((8, self.units // 8, self.width), BF16)],
            [*self.hidden, *self.cot],
            scalars=[self.ring_place],
        )
        self.ring_a.begin(grad)

    def wide(self):
        (grad,) = self.chain.direct(
            functools.partial(wide_grad_kernel, 2),
            [shape((8, self.width // 8, 2 * self.units), BF16)],
            [*self.normed2, *self.d_gate, *self.d_up],
            scalars=[self.ring_place],
        )
        self.ring_b.begin(grad)

    def putdown(self):
        (self.down_sum,) = self.ring_a.assemble([shape((8, self.units // 8, self.width), F32)], 0, 8)

    def putwide0(self):
        (self.gate_up_sum,) = self.ring_b.assemble([shape((2, 8, self.width // 8, self.units), F32)], 0, 6)

    def putwide1(self):
        (self.gate_up_sum,) = self.ring_b.assemble([self.gate_up_sum], 6, 8)

    def putlate(self):
        self.query_sum, self.out_sum = self.ring_e.assemble(
            [shape((8, self.width // 8, self.cols), F32), shape((8, self.cols // 8, self.width), F32)], 0, 8
        )

    def rows_back(self, side, chunks, lefts, weight, dims, extra):
        rows, count = chunks * self.quarter, len(lefts) // chunks
        return self.chain.direct(
            functools.partial(rows_kernel, side, 3, dims, count),
            [shape((rows, self.width), BF16)],
            [*lefts, weight, *extra],
            scratch=[pltpu.VMEM((rows, self.units), BF16)] * count,
        )[0]

    def dn(self, side, wide, extra=()):
        return self.rows_back(side, 1, wide[1:3], self.near_gate_up, NT, extra)

    def dnsib0(self):
        self.dn_from0 = swap_core(self.dn(1, self.wide0))

    def dnown0(self):
        self.dn_chip0 = self.dn(0, self.wide0, (self.dn_from0,))
        self.dn_x0 = swap_x(self.dn_chip0)

    def dnsib1(self):
        self.dn_from1 = swap_core(self.dn(1, self.wide1))

    def dnown1(self):
        self.dn_chip1 = self.dn(0, self.wide1, (self.dn_from1,))
        self.dn_x1 = swap_x(self.dn_chip1)

    def fo(self, side, wide, extra=()):
        return self.rows_back(side, 1, wide[:1], self.near_down, NN, extra)

    def fosib0(self):
        self.fo_from0 = swap_core(self.fo(1, self.wide0))

    def fosib1(self):
        self.fo_from1 = swap_core(self.fo(1, self.wide1))

    def foown0(self):
        self.fo_chip0 = self.fo(0, self.wide0, (self.fo_from0,))
        self.fo_x0 = swap_x(self.fo_chip0)

    def foown1(self):
        self.fo_chip1 = self.fo(0, self.wide1, (self.fo_from1,))
        self.fo_x1 = swap_x(self.fo_chip1)

    def nback(self, residual, on_chip, from_x, cot):
        q, w, c = self.quarter, self.width, 2 * self.cols
        outs = [shape((q, w), F32), shape((q, w), BF16), shape((q, c), BF16), shape((1, w), F32)]
        ins = [residual, on_chip, from_x, cot, self.gain2, self.out_w, self.out_sib]
        specs = [whole(a) for a in ins]
        specs[3] = pl.BlockSpec((q, w), lambda i: (0, 0))
        return self.chain.call(norm2_back_kernel, outs, ins, specs, [whole(o) for o in outs], far=(0, 1))

    def nback0(self):
        self.d_residual0, self.d_res_low0, self.d_heads0, self.norm2_part0 = self.nback(
            self.residual0, self.dn_chip0, self.dn_x0, self.cot[0]
        )

    def nback1(self):
        self.d_residual1, self.d_res_low1, self.d_heads1, self.norm2_part1 = self.nback(
            self.residual1, self.dn_chip1, self.dn_x1, self.cot[1]
        )

    def aback0(self):
        ins = [self.rot_q0, self.log0, self.d_heads0, self.far_keys, self.far_values, self.table]
        wide = shape((self.head_dim, self.length), F32)
        outs = [shape((self.quarter, 2 * self.cols), BF16), wide, wide]
        self.d_queries0, self.wide_keys, self.wide_values = self.chain.call(
            functools.partial(attend_back_kernel, self.scale, 0),
            outs,
            ins,
            [whole(a) for a in ins],
            [whole(a) for a in outs],
            scalars=[self.core[None]],
            far=(0,),
        )

    def aback1(self):
        ins = [self.rot_q1, self.log1, self.d_heads1, self.far_keys, self.far_values, self.table]
        ins += [self.wide_keys, self.wide_values]
        outs = [
            shape((self.quarter, 2 * self.cols), BF16),
            shape((self.half, 2 * self.head_dim), F32),
            shape((self.half, 2 * self.head_dim), BF16),
        ]
        self.d_queries1, self.kv_own, kv_sib = self.chain.call(
            functools.partial(attend_back_kernel, self.scale, 1),
            outs,
            ins,
            [whole(a) for a in ins],
            [whole(a) for a in outs],
            scalars=[self.core[None]],
            scratch=[pltpu.VMEM((self.length, self.head_dim), F32)] * 2
            + [pltpu.VMEM((self.head_dim, self.length), F32)] * 2,
        )
        self.d_queries = (self.d_queries0, self.d_queries1)
        self.kv_from = swap_core(kv_sib)

    def late(self):
        self.late_mine, other = self.chain.direct(
            functools.partial(late_grad_kernel, self.cols),
            [shape((8, self.width // 8, 2 * self.cols), t) for t in (F32, BF16)],
            [
                *self.far_normed1, *self.d_queries, self.head_out0, self.head_out1, self.d_res_low0, self.d_res_low1,
            ],
            scalars=[self.ring_place],
        )
        self.late_from = swap_core(other)

    def dn1(self, d_queries):
        tile = pl.BlockSpec((self.width // 3, self.cols), lambda i: (i, 0))
        return self.chain.call(
            d_normed1_kernel,
            [shape((self.quarter, self.width), BF16)],
            [d_queries, self.query_w, self.query_sib],
            [whole(d_queries), tile, tile],
            [pl.BlockSpec((self.quarter, self.width // 3), lambda i: (0, i))],
            grid=(3,),
        )[0]

    def dn10(self):
        self.dn1_chip0 = self.dn1(self.d_queries0)
        self.dn1_x0 = swap_x(self.dn1_chip0)

    def dn11(self):
        self.dn1_chip1 = self.dn1(self.d_queries1)
        self.dn1_x1 = swap_x(self.dn1_chip1)

    def kv(self):
        own, sent = self.chain.after(self.kv_own, self.kv_from)
        self.kv_chip = (own + sent.astype(F32)).astype(BF16)
        self.kv_x = swap_x(self.kv_chip)

    def kvpart(self):
        chip, from_x = self.chain.after(self.kv_chip, self.kv_x)
        self.d_kv = (chip.astype(F32) + from_x.astype(F32)).astype(BF16)
        mine = lax.dynamic_slice_in_dim(self.d_kv, self.chip * self.head_dim, self.head_dim, 1)
        normed1 = jnp.concatenate(self.far_normed1, 0)
        part = dot(normed1, mine, TN)
        mine = lax.dynamic_slice_in_dim(part, self.core * self.middle, self.middle, 0)
        other = lax.dynamic_slice_in_dim(part, (1 - self.core) * self.middle, self.middle, 0).astype(BF16)
        self.kv_grad = (mine + swap_core(other).astype(F32)).astype(BF16)

    def out(self, residual, chip, from_x):
        chip, from_x = self.chain.after(chip, from_x)
        own = (residual + (chip.astype(F32) + from_x.astype(F32))).astype(BF16)
        return own, swap_core(own)

    def out0(self):
        self.output_own0, self.output_sib0 = self.out(self.residual0, self.fo_chip0, self.fo_x0)

    def out1(self):
        self.output_own1, self.output_sib1 = self.out(self.residual1, self.fo_chip1, self.fo_x1)

    def input(self, j, on_chip, from_x, d_residual):
        q, w, d = self.quarter, self.width, 2 * self.head_dim
        block = pl.BlockSpec((q, w), lambda i, _: (0, 0))
        own, part = self.chain.call(
            norm1_back_kernel,
            [shape((q, w), BF16), shape((1, w), F32)],
            [self.x, on_chip, from_x, self.d_kv, d_residual, self.kv_w, self.gain1],
            [
                self.rows(1), block, block, pl.BlockSpec((q, d), lambda i, _: (j, 0)), block, whole(self.kv_w),
                whole(self.gain1),
            ],
            [block, pl.BlockSpec((1, w), lambda i, _: (0, 0))],
            scalars=[self.own[j : j + 1]],
            far_ins=(0, 5),
        )
        return own, swap_core(own), part

    def input0(self):
        self.input_own0, self.input_sib0, self.norm1_part0 = self.input(0, self.dn1_chip0, self.dn1_x0, self.d_residual0)

    def input1(self):
        self.input_own1, self.input_sib1, self.norm1_part1 = self.input(1, self.dn1_chip1, self.dn1_x1, self.d_residual1)

    def weave(self):
        ins = [self.output_own0, self.output_own1, self.output_sib0, self.output_sib1]
        ins += [self.input_own0, self.input_own1, self.input_sib0, self.input_sib1]
        self.block_output, self.input_grad = self.chain.direct(
            weave_kernel,
            [shape((self.length, self.width), BF16)] * 2,
            ins,
            scalars=[self.weave_places],
            far=(0, 1),
            scratch=[pltpu.SemaphoreType.DMA((8,))],
        )

    def sums(self):
        d = self.head_dim
        gains = jnp.concatenate([self.norm1_part0 + self.norm1_part1, self.norm2_part0 + self.norm2_part1], 0).reshape(-1, d).astype(BF16)
        self.small = jnp.concatenate([self.kv_grad, gains], 0)
        if self.n_dp & (self.n_dp - 1):
            self.small = lax.psum(self.small, "dp")

    def small_step(self, step):
        if self.n_dp & (self.n_dp - 1):
            return
        while step < self.n_dp:
            (small,) = self.chain.after(self.small)
            self.small = over_dp(small, step, self.n_dp).astype(BF16)
            if step < 4:
                return
            step *= 2

    def sums1(self):
        self.small_step(1)

    def sums2(self):
        self.small_step(2)

    def sums4(self):
        self.small_step(4)

    def sumscore(self):
        (small,) = self.chain.after(self.small)
        self.from_core = swap_core(small)
        self.small = small

    def sumschip(self):
        d, rows = self.head_dim, self.middle
        mine, other = self.chain.after(self.small, self.from_core)
        total = mine[rows:].astype(F32) + other[rows:].astype(F32)
        self.norm_sums = total.reshape(2, self.width)
        halves = jnp.stack([mine[:rows], other[:rows]])
        self.kv_column = jnp.where(self.core == 0, halves, halves[::-1]).reshape(self.width, d)
        self.kv_other = swap_x(self.kv_column)

    def sumsend(self):
        mine, other = self.chain.after(self.kv_column, self.kv_other)
        columns = jnp.stack([mine, other])
        columns = jnp.where(self.chip == 0, columns, columns[::-1])
        self.kv_out = jnp.concatenate([columns[0], columns[1]], 1).astype(F32)

    def E(self):
        (grad,) = self.chain.after((self.late_mine + self.late_from.astype(F32)).astype(BF16))
        self.ring_e.begin(grad)

    def e(self):
        self.ring_e.step()

    def a(self):
        self.ring_a.step()

    def b(self):
        self.ring_b.step()

    def results(self):
        return (
            self.block_output,
            self.input_grad,
            self.norm_sums[0],
            self.query_sum.reshape(self.width, self.cols),
            self.kv_out,
            self.out_sum.reshape(self.cols, self.width),
            self.norm_sums[1],
            self.gate_up_sum.reshape(2, self.width, self.units),
            self.down_sum.reshape(self.units, self.width),
        )


def solution(mesh):
    n_dp = mesh.shape["dp"]

    def local(*args):
        block = Block(n_dp, args)
        for name in ORDER:
            getattr(block, name)()
        return block.results()

    return jax.shard_map(
        local,
        mesh=mesh,
        in_specs=(
            P("dp", None),
            P(),
            P(None, "tensor"),
            P(),
            P("tensor", None),
            P(),
            P(None, None, "tensor"),
            P("tensor", None),
            P("dp", None),
        ),
        out_specs=(
            P("dp", None),
            P("dp", None),
            P(),
            P(None, "tensor"),
            P(),
            P("tensor", None),
            P(),
            P(None, None, "tensor"),
            P("tensor", None),
        ),
        check_vma=False,
    )
```

profile of v0, /device:TPU:0, one launch (start us, length us, event | category | flops | bytes accessed | tf_op | source)
XLA Modules:
  0.0 388.9 jit_solution(6960028387478485634)
XLA Ops:
  1.9 5.1 %shard_map.169 = (bf16[960,128]{1,0:T(8,128)(2,1)S(1)}, bf16[960,128]{1,0:T(8,128)(2,1)S(1)}, bf16[240,1536]{1,0:T(8,128)(2,1)S(1)}, bf16[240,1536]{1,0:T(8,128)...) custom-call(s32[1]{0:T(128)} %bitcast.refs_0_, ...), custom_call_target="tpu_custom_call" | custom-call | tf_op jit(solution)/shard_map/pallas_call | solution.py:121
  8.6 7.9 %shard_map.170 = (bf16[240,1536]{1,0:T(8,128)(2,1)S(1)}, bf16[240,768]{1,0:T(8,128)(2,1)}, bf16[240,768]{1,0:T(8,128)(2,1)}, f32[240,8]{1,0:T(8,128)}, bf16[240,...) custom-call(s32[1]{0:T(128)} %bitcast.refs_0_, s32[4]{0:T(128)S(1)} %add_add_fusion.1.refs_1_, ...), custom_call_target="tpu_custom_call" | custom-call | tf_op jit(solution)/shard_map/pallas_call | solution.py:95
  19.5 9.6 %shard_map.171 = (bf16[240,1536]{1,0:T(8,128)(2,1)S(1)}, bf16[240,768]{1,0:T(8,128)(2,1)}, bf16[240,768]{1,0:T(8,128)(2,1)}, f32[240,8]{1,0:T(8,128)}, bf16[240,...) custom-call(s32[1]{0:T(128)} %bitcast.1.refs_0_, ...), custom_call_target="tpu_custom_call" | custom-call | tf_op jit(solution)/shard_map/pallas_call | solution.py:95
  33.0 3.8 collective-permute-done.2.refs_3_
  42.9 4.1 %shard_map.175 = (bf16[480,1152]{1,0:T(8,128)(2,1)S(1)}, bf16[480,1152]{1,0:T(8,128)(2,1)S(1)}, bf16[480,1152]{1,0:T(8,128)(2,1)S(1)}, bf16[480,1536]{1,0:T(8,128)(2,1)S(1)}, f32[8,128]{1,0:T(8,128)S(1)}) custom-call(bf16[128,1536]{1,0:T(8,128)(2,1)S(1)} %get-tuple-element.286.refs_0_, bf16[112,1536]{1,0:T(8,128)(2,1)S(1)} %get-tuple-element.287.refs_1_, ...), custom_call_target="tpu_custom_call" | custom-call | tf_op jit(solution)/shard_map/pallas_call | solution.py:121
  63.8 5.9 %shard_map.178 = (bf16[480,1152]{1,0:T(8,128)(2,1)S(1)}, bf16[480,1152]{1,0:T(8,128)(2,1)S(1)}, bf16[480,1152]{1,0:T(8,128)(2,1)S(1)}, bf16[480,1536]{1,0:T(8,128)(2,1)S(1)}, f32[8,128]{1,0:T(8,128)S(1)}) custom-call(bf16[128,1536]{1,0:T(8,128)(2,1)} %get-tuple-element.299.refs_0_, bf16[112,1536]{1,0:T(8,128)(2,1)} %get-tuple-element.300.refs_1_, ...), custom_call_target="tpu_custom_call" | custom-call | tf_op jit(solution)/shard_map/pallas_call | solution.py:121
  69.7 9.1 %shard_map.179 = (bf16[8,192,2304]{2,1,0:T(8,128)(2,1)S(1)}, f32[8,128]{1,0:T(8,128)S(1)}) custom-call(s32[2]{0:T(128)S(1)} %pad_add_fusion.refs_0_, bf16[480,1536]{1,0:T(8,128)(2,1)S(1)} %copy-done.37, bf16[480,1536]{1,0:T(8,128)(2,1)S(1)} %get-tuple-element.305.refs_2_, bf16[480,1152]{1,0:T(8,128)(2,1)S(1)} %copy-done.21, ...), custom_call_target="tpu_custom_call" | custom-call | tf_op jit(solution)/shard_map/pallas_call | solution.py:121
  83.8 4.5 %shard_map.181 = (bf16[8,144,1536]{2,1,0:T(8,128)(2,1)S(1)}, f32[8,128]{1,0:T(8,128)S(1)}) custom-call(s32[2]{0:T(128)S(1)} %pad_add_fusion.refs_0_, bf16[480,1152]{1,0:T(8,128)(2,1)S(1)} %copy-done.18, bf16[480,1152]{1,0:T(8,128)(2,1)S(1)} %get-tuple-element.303.refs_2_.refs_0_, bf16[480,1536]{1,0:T(8,128)(2,1)S(1)} %copy-done.14, ...), custom_call_target="tpu_custom_call" | custom-call | tf_op jit(solution)/shard_map/pallas_call | solution.py:121
  92.6 4.5 %collective-permute-done.11 = bf16[144,1536]{1,0:T(8,128)(2,1)S(1)} collective-permute-done((bf16[144,1536]{1,0:T(8,128)(2,1)S(1)}, bf16[144,1536]{1,0:T(8,128)(2,1)S(1)}, u32[]{:S(2)}, u32[]{:S(2)}) %collective-permute-start.11) | collective-permute-done | bytes 442400 | tf_op jit(solution)/shard_map/ppermute | solution.py:512
  110.1 5.0 %collective-permute-done.10 = bf16[192,2304]{1,0:T(8,128)(2,1)S(1)} collective-permute-done((bf16[192,2304]{1,0:T(8,128)(2,1)S(1)}, bf16[192,2304]{1,0:T(8,128)(2,1)S(1)}, u32[]{:S(2)}, u32[]{:S(2)}) %collective-permute-start.10) | collective-permute-done | bytes 884768 | tf_op jit(solution)/shard_map/ppermute | solution.py:512
  115.3 4.5 %collective-permute-done.17 = bf16[144,1536]{1,0:T(8,128)(2,1)S(1)} collective-permute-done((bf16[144,1536]{1,0:T(8,128)(2,1)S(1)}, bf16[144,1536]{1,0:T(8,128)(2,1)S(1)}, u32[]{:S(2)}, u32[]{:S(2)}) %collective-permute-start.17) | collective-permute-done | bytes 442400 | tf_op jit(solution)/shard_map/ppermute | solution.py:512
  130.6 3.5 shard_map.185
  134.1 5.8 %collective-permute-done.15.refs_2_ = bf16[240,1536]{1,0:T(8,128)(2,1)S(1)} collective-permute-done((bf16[240,1536]{1,0:T(8,128)(2,1)S(1)}, bf16[240,1536]{1,0:T(8,128)(2,1)S(1)}, u32[]{:S(2)}, u32[]{:S(2)}) %collective-permute-start.15) | collective-permute-done | bytes 737312 | tf_op jit(solution)/shard_map/ppermute | solution.py:66
  146.4 5.9 %shard_map.187 = (bf16[240,768]{1,0:T(8,128)(2,1)S(1)}, f32[480,256]{1,0:T(8,128)S(1)}, bf16[480,256]{1,0:T(8,128)(2,1)S(1)}, f32[8,128]{1,0:T(8,128)S(1)}) custom-call(s32[1]{0:T(128)} %bitcast.refs_0_, bf16[240,768]{1,0:T(8,128)(2,1)S(1)} %copy-done.71, f32[240,8]{1,0:T(8,128)S(1)} %copy-done.83, bf16[240,768]{1,0:T(8,128)(2,1)S(1)} %get-tuple-element.362.refs_3_, ...), custom_call_target="tpu_custom_call" | custom-call | tf_op jit(solution)/shard_map/pallas_call | solution.py:95
  152.5 8.2 %collective-permute-done.19 = bf16[192,2304]{1,0:T(8,128)(2,1)S(1)} collective-permute-done((bf16[192,2304]{1,0:T(8,128)(2,1)S(1)}, bf16[192,2304]{1,0:T(8,128)(2,1)S(1)}, u32[]{:S(2)}, u32[]{:S(2)}) %collective-permute-start.19) | collective-permute-done | bytes 884768 | tf_op jit(solution)/shard_map/ppermute | solution.py:512
  161.0 3.6 shard_map.188
  169.7 3.4 collective-permute-done.23
  175.1 7.5 %collective-permute-done.22 = bf16[192,2304]{1,0:T(8,128)(2,1)S(1)} collective-permute-done((bf16[192,2304]{1,0:T(8,128)(2,1)S(1)}, bf16[192,2304]{1,0:T(8,128)(2,1)S(1)}, u32[]{:S(2)}, u32[]{:S(2)}) %collective-permute-start.22) | collective-permute-done | bytes 884768 | tf_op jit(solution)/shard_map/ppermute | solution.py:512
  209.5 6.8 %collective-permute-done.32 = bf16[192,768]{1,0:T(8,128)(2,1)} collective-permute-done((bf16[192,768]{1,0:T(8,128)(2,1)}, bf16[192,768]{1,0:T(8,128)(2,1)}, u32[]{:S(2)}, u32[]{:S(2)}) %collective-permute-start.32) | collective-permute-done | bytes 294944 | tf_op jit(solution)/shard_map/ppermute | solution.py:512
  221.1 3.2 collective-permute-done.33
  242.4 4.0 %collective-permute-done.37.refs_2_ = bf16[192,2304]{1,0:T(8,128)(2,1)} collective-permute-done((bf16[192,2304]{1,0:T(8,128)(2,1)S(1)}, bf16[192,2304]{1,0:T(8,128)(2,1)}, u32[]{:S(2)}, u32[]{:S(2)}) %collective-permute-start.37) | collective-permute-done | bytes 884768 | tf_op jit(solution)/shard_map/ppermute | solution.py:512
  254.6 3.3 shard_map.195
  260.8 6.9 %collective-permute-done.40.refs_3_ = bf16[192,2304]{1,0:T(8,128)(2,1)} collective-permute-done((bf16[192,2304]{1,0:T(8,128)(2,1)}, bf16[192,2304]{1,0:T(8,128)(2,1)}, u32[]{:S(2)}, u32[]{:S(2)}) %collective-permute-start.40) | collective-permute-done | bytes 884768 | tf_op jit(solution)/shard_map/ppermute | solution.py:512
  282.8 6.6 %collective-permute-done.50 = bf16[792,128]{1,0:T(8,128)(2,1)S(1)} collective-permute-done((bf16[792,128]{1,0:T(8,128)(2,1)S(1)}, bf16[792,128]{1,0:T(8,128)(2,1)S(1)}, u32[]{:S(2)}, u32[]{:S(2)}) %collective-permute-start.50) | collective-permute-done | bytes 202784 | tf_op jit(solution)/shard_map/ppermute | solution.py:559
  289.5 4.7 %collective-permute-start.56 = (bf16[792,128]{1,0:T(8,128)(2,1)S(1)}, bf16[792,128]{1,0:T(8,128)(2,1)S(1)}, u32[]{:S(2)}, u32[]{:S(2)}) collective-permute-start(bf16[792,128]{1,0:T(8,128)(2,1)S(1)} %add_convert_fusion.6), channel_id=1, source_target_pairs={{0,16},{4,20},{8,24},{12,28},{16,0},{20,4},{24,8},{28,12},{1,17},{... | collective-permute-start | bytes 608264 | tf_op jit(solution)/shard_map/ppermute | solution.py:559
  297.9 4.5 %collective-permute-done.56 = bf16[792,128]{1,0:T(8,128)(2,1)S(1)} collective-permute-done((bf16[792,128]{1,0:T(8,128)(2,1)S(1)}, bf16[792,128]{1,0:T(8,128)(2,1)S(1)}, u32[]{:S(2)}, u32[]{:S(2)}) %collective-permute-start.56) | collective-permute-done | bytes 202784 | tf_op jit(solution)/shard_map/ppermute | solution.py:559
  304.0 11.4 %collective-permute-done.53.refs_3_ = bf16[192,768]{1,0:T(8,128)(2,1)S(1)} collective-permute-done((bf16[192,768]{1,0:T(8,128)(2,1)S(1)}, bf16[192,768]{1,0:T(8,128)(2,1)S(1)}, u32[]{:S(2)}, u32[]{:S(2)}) %collective-permute-start.53) | collective-permute-done | bytes 294944 | tf_op jit(solution)/shard_map/ppermute | solution.py:512
  318.9 3.9 %collective-permute-done.54.refs_4_ = bf16[192,768]{1,0:T(8,128)(2,1)S(1)} collective-permute-done((bf16[192,768]{1,0:T(8,128)(2,1)S(1)}, bf16[192,768]{1,0:T(8,128)(2,1)S(1)}, u32[]{:S(2)}, u32[]{:S(2)}) %collective-permute-start.54) | collective-permute-done | bytes 294944 | tf_op jit(solution)/shard_map/ppermute | solution.py:512
  339.4 4.2 %shard_map.197 = (bf16[960,1536]{1,0:T(8,128)(2,1)}, bf16[960,1536]{1,0:T(8,128)(2,1)}, f32[8,128]{1,0:T(8,128)S(1)}) custom-call(s32[4]{0:T(128)S(1)} %add_add_fusion.refs_0_, bf16[240,1536]{1,0:T(8,128)(2,1)S(1)} %add_convert_fusion.2.refs_1_, bf16[240,1536]{1,0:T(8,128)(2,1)S(1)} %add_convert_fusion.1.refs_2_, ...), custom_call_target="tpu_custom_call" | custom-call | tf_op jit(solution)/shard_map/pallas_call | solution.py:121
  357.3 6.1 %shard_map.198 = (f32[8,144,1536]{2,1,0:T(8,128)}, f32[8,128]{1,0:T(8,128)S(1)}) custom-call(s32[2]{0:T(128)S(1)} %copy-done.86, bf16[144,1536]{1,0:T(8,128)(2,1)S(1)} %copy-done.35, bf16[144,1536]{1,0:T(8,128)(2,1)S(1)} %copy-done.68, bf16[144,1536]{1,0:T(8,128)(2,1)S(1)} %copy-done.70, bf16[144,1536]{1,0:T(8,128)(2,1)} %collective-permute-done.38.refs_4_, ...), custom_call_target="tpu_custom_call" | custom-call | tf_op jit(solution)/shard_map/pallas_call | solution.py:95
  371.8 7.1 %shard_map.199 = (f32[2,8,192,1152]{3,2,1,0:T(8,128)}, f32[8,128]{1,0:T(8,128)S(1)}) custom-call(s32[2]{0:T(128)S(1)} %copy-done.86, bf16[192,2304]{1,0:T(8,128)(2,1)S(1)} %copy-done.33, bf16[192,2304]{1,0:T(8,128)(2,1)} %collective-permute-done.37.refs_2_, bf16[192,2304]{1,0:T(8,128)(2,1)} %collective-permute-done.40.refs_3_, ...), custom_call_target="tpu_custom_call" | custom-call | tf_op jit(solution)/shard_map/pallas_call | solution.py:95
  381.6 4.2 %shard_map.200 = (f32[8,192,384]{2,1,0:T(8,128)}, f32[8,48,1536]{2,1,0:T(8,128)}, f32[8,128]{1,0:T(8,128)S(1)}) custom-call(s32[2]{0:T(128)S(1)} %copy-done.86, bf16[192,768]{1,0:T(8,128)(2,1)S(1)} %copy-done.43, bf16[192,768]{1,0:T(8,128)(2,1)S(1)} %copy-done.76, bf16[192,768]{1,0:T(8,128)(2,1)S(1)} %copy-done.78, bf16[192,768]{1,0:T(8,128)(2,1)S(1)} %copy-done.80, ...), custom_call_target="tpu_custom_call" | custom-call | tf_op jit(solution)/shard_map/pallas_call | solution.py:95
  (407 shorter events, 207.2 us)
Async XLA Ops:
  16.5 20.2 %collective-permute-start.2 = (bf16[240,1536]{1,0:T(8,128)(2,1)S(1)}, bf16[240,1536]{1,0:T(8,128)(2,1)S(1)}, u32[]{:S(2)}, u32[]{:S(2)}) collective-permute-start(bf16[240,1536]{1,0:T(8,128)(2,1)S(1)} %get-tuple-element.277.refs_2_), channel_id=1, source_target_pairs={{0,2},{1,3},{2,0},{3,1},{4,6},{5,7},{6,4},{7,5},{8,10},{9,11},{10,... | collective-permute-start | bytes 2211848 | tf_op jit(solution)/shard_map/ppermute | solution.py:66
  29.1 23.2 %collective-permute-start.5 = (bf16[240,1536]{1,0:T(8,128)(2,1)S(1)}, bf16[240,1536]{1,0:T(8,128)(2,1)S(1)}, u32[]{:S(2)}, u32[]{:S(2)}) collective-permute-start(bf16[240,1536]{1,0:T(8,128)(2,1)S(1)} %get-tuple-element.294.refs_2_), channel_id=1, source_target_pairs={{0,2},{1,3},{2,0},{3,1},{4,6},{5,7},{6,4},{7,5},{8,10},{9,11},{10,... | collective-permute-start | bytes 2211848 | tf_op jit(solution)/shard_map/ppermute | solution.py:66
  56.9 24.6 %collective-permute-start.9 = (bf16[240,1536]{1,0:T(8,128)(2,1)}, bf16[240,1536]{1,0:T(8,128)(2,1)S(1)}, u32[]{:S(2)}, u32[]{:S(2)}) collective-permute-start(bf16[240,1536]{1,0:T(8,128)(2,1)} %copy-done.94), channel_id=1, source_target_pairs={{0,1},{1,0},{2,3},{3,2},{4,5},{5,4},{6,7},{7,6},{8,9},{9,8},{10,11... | collective-permute-start | bytes 2211848 | tf_op jit(solution)/shard_map/ppermute | solution.py:62
  99.4 15.7 %collective-permute-start.10 = (bf16[192,2304]{1,0:T(8,128)(2,1)S(1)}, bf16[192,2304]{1,0:T(8,128)(2,1)S(1)}, u32[]{:S(2)}, u32[]{:S(2)}) collective-permute-start(bf16[192,2304]{1,0:T(8,128)(2,1)S(1)} %fusion.6), channel_id=1, source_target_pairs={{0,8},{8,16},{16,24},{24,28},{28,20},{20,12},{12,4},{4,0},{5,13},{... | collective-permute-start | bytes 2654216 | tf_op jit(solution)/shard_map/ppermute | solution.py:512
  103.3 21.8 %collective-permute-start.16 = (bf16[240,1536]{1,0:T(8,128)(2,1)S(1)}, bf16[240,1536]{1,0:T(8,128)(2,1)S(1)}, u32[]{:S(2)}, u32[]{:S(2)}) collective-permute-start(bf16[240,1536]{1,0:T(8,128)(2,1)S(1)} %get-tuple-element.336.refs_1_), channel_id=1, source_target_pairs={{0,2},{1,3},{2,0},{3,1},{4,6},{5,7},{6,4},{7,5},{8,10},{9,11},{10,... | collective-permute-start | bytes 2211848 | tf_op jit(solution)/shard_map/ppermute | solution.py:66
  122.1 20.3 %collective-permute-start.14 = (bf16[192,2304]{1,0:T(8,128)(2,1)S(1)}, bf16[192,2304]{1,0:T(8,128)(2,1)S(1)}, u32[]{:S(2)}, u32[]{:S(2)}) collective-permute-start(bf16[192,2304]{1,0:T(8,128)(2,1)S(1)} %fusion.5), channel_id=1, source_target_pairs={{0,8},{8,16},{16,24},{24,28},{28,20},{20,12},{12,4},{4,0},{5,13},{... | collective-permute-start | bytes 2654216 | tf_op jit(solution)/shard_map/ppermute | solution.py:512
  123.7 16.2 %collective-permute-start.15 = (bf16[240,1536]{1,0:T(8,128)(2,1)S(1)}, bf16[240,1536]{1,0:T(8,128)(2,1)S(1)}, u32[]{:S(2)}, u32[]{:S(2)}) collective-permute-start(bf16[240,1536]{1,0:T(8,128)(2,1)S(1)} %get-tuple-element.333.refs_1_), channel_id=1, source_target_pairs={{0,2},{1,3},{2,0},{3,1},{4,6},{5,7},{6,4},{7,5},{8,10},{9,11},{10,... | collective-permute-start | bytes 2211848 | tf_op jit(solution)/shard_map/ppermute | solution.py:66
  144.8 16.0 %collective-permute-start.19 = (bf16[192,2304]{1,0:T(8,128)(2,1)S(1)}, bf16[192,2304]{1,0:T(8,128)(2,1)S(1)}, u32[]{:S(2)}, u32[]{:S(2)}) collective-permute-start(bf16[192,2304]{1,0:T(8,128)(2,1)S(1)} %fusion.4), channel_id=1, source_target_pairs={{0,8},{8,16},{16,24},{24,28},{28,20},{20,12},{12,4},{4,0},{5,13},{... | collective-permute-start | bytes 2654216 | tf_op jit(solution)/shard_map/ppermute | solution.py:512
  164.7 29.6 %collective-permute-start.29 = (bf16[8,192,768]{2,1,0:T(8,128)(2,1)S(1)}, bf16[8,192,768]{2,1,0:T(8,128)(2,1)S(1)}, u32[]{:S(2)}, u32[]{:S(2)}) collective-permute-start(bf16[8,192,768]{2,1,0:T(8,128)(2,1)S(1)} %get-tuple-element.406), channel_id=1, source_target_pairs={{0,1},{1,0},{2,3},{3,2},{4,5},{5,4},{6,7},{7,6},{8,9},{9,8},{10,11... | collective-permute-start | bytes 7077896 | tf_op jit(solution)/shard_map/ppermute | solution.py:62
  166.6 16.0 %collective-permute-start.22 = (bf16[192,2304]{1,0:T(8,128)(2,1)S(1)}, bf16[192,2304]{1,0:T(8,128)(2,1)S(1)}, u32[]{:S(2)}, u32[]{:S(2)}) collective-permute-start(bf16[192,2304]{1,0:T(8,128)(2,1)S(1)} %fusion.3), channel_id=1, source_target_pairs={{0,8},{8,16},{16,24},{24,28},{28,20},{20,12},{12,4},{4,0},{5,13},{... | collective-permute-start | bytes 2654216 | tf_op jit(solution)/shard_map/ppermute | solution.py:512
  173.2 18.7 %collective-permute-start.26 = (bf16[144,1536]{1,0:T(8,128)(2,1)S(1)}, bf16[144,1536]{1,0:T(8,128)(2,1)S(1)}, u32[]{:S(2)}, u32[]{:S(2)}) collective-permute-start(bf16[144,1536]{1,0:T(8,128)(2,1)S(1)} %fusion.11.refs_1_), channel_id=1, source_target_pairs={{0,8},{8,16},{16,24},{24,28},{28,20},{20,12},{12,4},{4,0},{5,13},{... | collective-permute-start | bytes 1327112 | tf_op jit(solution)/shard_map/ppermute | solution.py:512
  199.8 19.6 %collective-permute-start.35 = (bf16[192,2304]{1,0:T(8,128)(2,1)}, bf16[192,2304]{1,0:T(8,128)(2,1)}, u32[]{:S(2)}, u32[]{:S(2)}) collective-permute-start(bf16[192,2304]{1,0:T(8,128)(2,1)} %fusion.1), channel_id=1, source_target_pairs={{0,8},{8,16},{16,24},{24,28},{28,20},{20,12},{12,4},{4,0},{5,13},{... | collective-permute-start | bytes 2654216 | tf_op jit(solution)/shard_map/ppermute | solution.py:512
  206.2 14.8 %collective-permute-start.34 = (bf16[144,1536]{1,0:T(8,128)(2,1)}, bf16[144,1536]{1,0:T(8,128)(2,1)S(1)}, u32[]{:S(2)}, u32[]{:S(2)}) collective-permute-start(bf16[144,1536]{1,0:T(8,128)(2,1)} %copy-done.67), channel_id=1, source_target_pairs={{0,8},{8,16},{16,24},{24,28},{28,20},{20,12},{12,4},{4,0},{5,13},{... | collective-permute-start | bytes 1327112 | tf_op jit(solution)/shard_map/ppermute | solution.py:512
  208.0 21.7 %collective-permute-start.28 = (bf16[240,1536]{1,0:T(8,128)(2,1)}, bf16[240,1536]{1,0:T(8,128)(2,1)S(1)}, u32[]{:S(2)}, u32[]{:S(2)}) collective-permute-start(bf16[240,1536]{1,0:T(8,128)(2,1)} %copy-done.59), channel_id=1, source_target_pairs={{0,2},{1,3},{2,0},{3,1},{4,6},{5,7},{6,4},{7,5},{8,10},{9,11},{10,... | collective-permute-start | bytes 2211848 | tf_op jit(solution)/shard_map/ppermute | solution.py:66
  209.5 25.9 %collective-permute-start.25 = (bf16[240,1536]{1,0:T(8,128)(2,1)}, bf16[240,1536]{1,0:T(8,128)(2,1)S(1)}, u32[]{:S(2)}, u32[]{:S(2)}) collective-permute-start(bf16[240,1536]{1,0:T(8,128)(2,1)} %copy-done.93), channel_id=1, source_target_pairs={{0,1},{1,0},{2,3},{3,2},{4,5},{5,4},{6,7},{7,6},{8,9},{9,8},{10,11... | collective-permute-start | bytes 2211848 | tf_op jit(solution)/shard_map/ppermute | solution.py:62
  229.7 16.7 %collective-permute-start.37 = (bf16[192,2304]{1,0:T(8,128)(2,1)S(1)}, bf16[192,2304]{1,0:T(8,128)(2,1)}, u32[]{:S(2)}, u32[]{:S(2)}) collective-permute-start(bf16[192,2304]{1,0:T(8,128)(2,1)S(1)} %fusion.refs_1_), channel_id=1, source_target_pairs={{0,8},{8,16},{16,24},{24,28},{28,20},{20,12},{12,4},{4,0},{5,13},{... | collective-permute-start | bytes 2654216 | tf_op jit(solution)/shard_map/ppermute | solution.py:512
  235.4 19.2 %collective-permute-start.44 = (bf16[240,1536]{1,0:T(8,128)(2,1)S(1)}, bf16[240,1536]{1,0:T(8,128)(2,1)S(1)}, u32[]{:S(2)}, u32[]{:S(2)}) collective-permute-start(bf16[240,1536]{1,0:T(8,128)(2,1)S(1)} %get-tuple-element.449.refs_2_), channel_id=1, source_target_pairs={{0,2},{1,3},{2,0},{3,1},{4,6},{5,7},{6,4},{7,5},{8,10},{9,11},{10,... | collective-permute-start | bytes 2211848 | tf_op jit(solution)/shard_map/ppermute | solution.py:66
  241.1 39.3 %collective-permute-start.51 = (bf16[240,1536]{1,0:T(8,128)(2,1)}, bf16[240,1536]{1,0:T(8,128)(2,1)}, u32[]{:S(2)}, u32[]{:S(2)}) collective-permute-start(bf16[240,1536]{1,0:T(8,128)(2,1)} %get-tuple-element.471), channel_id=1, source_target_pairs={{0,1},{1,0},{2,3},{3,2},{4,5},{5,4},{6,7},{7,6},{8,9},{9,8},{10,11... | collective-permute-start | bytes 2211848 | tf_op jit(solution)/shard_map/ppermute | solution.py:62
  241.9 18.9 %collective-permute-start.41 = (bf16[144,1536]{1,0:T(8,128)(2,1)}, bf16[144,1536]{1,0:T(8,128)(2,1)}, u32[]{:S(2)}, u32[]{:S(2)}) collective-permute-start(bf16[144,1536]{1,0:T(8,128)(2,1)} %collective-permute-done.38.refs_4_), channel_id=1, source_target_pairs={{0,8},{8,16},{16,24},{24,28},{28,20},{20,12},{12,4},{4,0},{5,13},{... | collective-permute-start | bytes 1327112 | tf_op jit(solution)/shard_map/ppermute | solution.py:512
  253.1 14.7 %collective-permute-start.40 = (bf16[192,2304]{1,0:T(8,128)(2,1)}, bf16[192,2304]{1,0:T(8,128)(2,1)}, u32[]{:S(2)}, u32[]{:S(2)}) collective-permute-start(bf16[192,2304]{1,0:T(8,128)(2,1)} %collective-permute-done.37.refs_2_), channel_id=1, source_target_pairs={{0,8},{8,16},{16,24},{24,28},{28,20},{20,12},{12,4},{4,0},{5,13},{... | collective-permute-start | bytes 2654216 | tf_op jit(solution)/shard_map/ppermute | solution.py:512
  271.1 25.7 %collective-permute-start.45 = (bf16[192,2304]{1,0:T(8,128)(2,1)}, bf16[192,2304]{1,0:T(8,128)(2,1)S(1)}, u32[]{:S(2)}, u32[]{:S(2)}) collective-permute-start(bf16[192,2304]{1,0:T(8,128)(2,1)} %collective-permute-done.40.refs_3_), channel_id=1, source_target_pairs={{0,8},{8,16},{16,24},{24,28},{28,20},{20,12},{12,4},{4,0},{5,13},{... | collective-permute-start | bytes 2654216 | tf_op jit(solution)/shard_map/ppermute | solution.py:512
  272.7 31.2 %collective-permute-start.36 = (bf16[240,1536]{1,0:T(8,128)(2,1)}, bf16[240,1536]{1,0:T(8,128)(2,1)S(1)}, u32[]{:S(2)}, u32[]{:S(2)}) collective-permute-start(bf16[240,1536]{1,0:T(8,128)(2,1)} %copy-done.50), channel_id=1, source_target_pairs={{0,2},{1,3},{2,0},{3,1},{4,6},{5,7},{6,4},{7,5},{8,10},{9,11},{10,... | collective-permute-start | bytes 2211848 | tf_op jit(solution)/shard_map/ppermute | solution.py:66
  280.3 16.4 %collective-permute-start.49 = (bf16[192,768]{1,0:T(8,128)(2,1)S(1)}, bf16[192,768]{1,0:T(8,128)(2,1)S(1)}, u32[]{:S(2)}, u32[]{:S(2)}) collective-permute-start(bf16[192,768]{1,0:T(8,128)(2,1)S(1)} %fusion.18.refs_1_), channel_id=1, source_target_pairs={{0,8},{8,16},{16,24},{24,28},{28,20},{20,12},{12,4},{4,0},{5,13},{... | collective-permute-start | bytes 884744 | tf_op jit(solution)/shard_map/ppermute | solution.py:512
  294.2 21.2 %collective-permute-start.55 = (bf16[144,1536]{1,0:T(8,128)(2,1)}, bf16[144,1536]{1,0:T(8,128)(2,1)}, u32[]{:S(2)}, u32[]{:S(2)}) collective-permute-start(bf16[144,1536]{1,0:T(8,128)(2,1)} %collective-permute-done.41.refs_5_), channel_id=1, source_target_pairs={{0,8},{8,16},{16,24},{24,28},{28,20},{20,12},{12,4},{4,0},{5,13},{... | collective-permute-start | bytes 1327112 | tf_op jit(solution)/shard_map/ppermute | solution.py:512
  296.8 29.1 %collective-permute-start.62 = (bf16[192,2304]{1,0:T(8,128)(2,1)S(1)}, bf16[192,2304]{1,0:T(8,128)(2,1)}, u32[]{:S(2)}, u32[]{:S(2)}) collective-permute-start(bf16[192,2304]{1,0:T(8,128)(2,1)S(1)} %collective-permute-done.45.refs_4_), channel_id=1, source_target_pairs={{0,8},{8,16},{16,24},{24,28},{28,20},{20,12},{12,4},{4,0},{5,13},{... | collective-permute-start | bytes 2654216 | tf_op jit(solution)/shard_map/ppermute | solution.py:512
  297.0 18.4 %collective-permute-start.53 = (bf16[192,768]{1,0:T(8,128)(2,1)S(1)}, bf16[192,768]{1,0:T(8,128)(2,1)S(1)}, u32[]{:S(2)}, u32[]{:S(2)}) collective-permute-start(bf16[192,768]{1,0:T(8,128)(2,1)S(1)} %collective-permute-done.49.refs_2_), channel_id=1, source_target_pairs={{0,8},{8,16},{16,24},{24,28},{28,20},{20,12},{12,4},{4,0},{5,13},{... | collective-permute-start | bytes 884744 | tf_op jit(solution)/shard_map/ppermute | solution.py:512
  302.3 20.5 %collective-permute-start.52 = (bf16[240,1536]{1,0:T(8,128)(2,1)S(1)}, bf16[240,1536]{1,0:T(8,128)(2,1)S(1)}, u32[]{:S(2)}, u32[]{:S(2)}) collective-permute-start(bf16[240,1536]{1,0:T(8,128)(2,1)S(1)} %get-tuple-element.489), channel_id=1, source_target_pairs={{0,2},{1,3},{2,0},{3,1},{4,6},{5,7},{6,4},{7,5},{8,10},{9,11},{10,... | collective-permute-start | bytes 2211848 | tf_op jit(solution)/shard_map/ppermute | solution.py:66
  303.9 24.7 %collective-permute-start.60 = (bf16[240,1536]{1,0:T(8,128)(2,1)S(1)}, bf16[240,1536]{1,0:T(8,128)(2,1)S(1)}, u32[]{:S(2)}, u32[]{:S(2)}) collective-permute-start(bf16[240,1536]{1,0:T(8,128)(2,1)S(1)} %copy-done.57), channel_id=1, source_target_pairs={{0,1},{1,0},{2,3},{3,2},{4,5},{5,4},{6,7},{7,6},{8,9},{9,8},{10,11... | collective-permute-start | bytes 2211848 | tf_op jit(solution)/shard_map/ppermute | solution.py:62
  325.8 21.0 %collective-permute-start.67 = (bf16[192,2304]{1,0:T(8,128)(2,1)}, bf16[192,2304]{1,0:T(8,128)(2,1)}, u32[]{:S(2)}, u32[]{:S(2)}) collective-permute-start(bf16[192,2304]{1,0:T(8,128)(2,1)} %collective-permute-done.62.refs_5_), channel_id=1, source_target_pairs={{0,8},{8,16},{16,24},{24,28},{28,20},{20,12},{12,4},{4,0},{5,13},{... | collective-permute-start | bytes 2654216 | tf_op jit(solution)/shard_map/ppermute | solution.py:512
  333.8 18.9 %collective-permute-start.64 = (bf16[192,768]{1,0:T(8,128)(2,1)}, bf16[192,768]{1,0:T(8,128)(2,1)S(1)}, u32[]{:S(2)}, u32[]{:S(2)}) collective-permute-start(bf16[192,768]{1,0:T(8,128)(2,1)} %copy-done.81), channel_id=1, source_target_pairs={{0,8},{8,16},{16,24},{24,28},{28,20},{20,12},{12,4},{4,0},{5,13},{... | collective-permute-start | bytes 884744 | tf_op jit(solution)/shard_map/ppermute | solution.py:512
  346.9 18.5 %collective-permute-start.71 = (bf16[192,2304]{1,0:T(8,128)(2,1)}, bf16[192,2304]{1,0:T(8,128)(2,1)S(1)}, u32[]{:S(2)}, u32[]{:S(2)}) collective-permute-start(bf16[192,2304]{1,0:T(8,128)(2,1)} %collective-permute-done.67.refs_6_), channel_id=1, source_target_pairs={{0,8},{8,16},{16,24},{24,28},{28,20},{20,12},{12,4},{4,0},{5,13},{... | collective-permute-start | bytes 2654216 | tf_op jit(solution)/shard_map/ppermute | solution.py:512
  365.3 20.5 %collective-permute-start.72 = (bf16[192,2304]{1,0:T(8,128)(2,1)S(1)}, bf16[192,2304]{1,0:T(8,128)(2,1)S(1)}, u32[]{:S(2)}, u32[]{:S(2)}) collective-permute-start(bf16[192,2304]{1,0:T(8,128)(2,1)S(1)} %collective-permute-done.71.refs_1_), channel_id=1, source_target_pairs={{0,8},{8,16},{16,24},{24,28},{28,20},{20,12},{12,4},{4,0},{5,13},{... | collective-permute-start | bytes 2654216 | tf_op jit(solution)/shard_map/ppermute | solution.py:512
  (144 other events, 1491.2 us)
where the time goes:
time: 397 us; the launch traced here: 389 us
  Pallas kernels  121 us (30%)
  waiting for transfers between devices  118 us (30%)
  starting transfers between devices  105 us (26%)
  local copies, waits for them, and re-layouts  23.4 us (6%)
  other arithmetic  18.6 us (5%)
    ppermute x42, waiting for transfers between devices, send(): self.arrived = lax.ppermute(self.travelling, ('dp', 'tensor'), ring_pairs())  88.8 us
    ppermute x42, starting transfers between devices, send(): self.arrived = lax.ppermute(self.travelling, ('dp', 'tensor'), ring_pairs())  78.3 us
    pallas_call x14, Pallas kernels, call(): pl.pallas_call(run, out_shape=outs + [shape((8, 128), F32)], grid_spec=pl...  60.7 us
    pallas_call x19, Pallas kernels, direct(): pl.pallas_call(run, out_shape=[pltpu.HBM(o.shape, o.dtype) if i in far el...  60.2 us
    unnamed x206, local copies, waits for them, and re-layouts  20.2 us
    ppermute x10, starting transfers between devices, swap_x(): return lax.ppermute(field, 'tensor', [(i, i ^ 2) for i in range(4)])  15.2 us
    ppermute x10, waiting for transfers between devices, swap_x(): return lax.ppermute(field, 'tensor', [(i, i ^ 2) for i in range(4)])  13.6 us
    convert_element_type x21, other arithmetic, step(): (self.travelling.astype(F32) + mine).astype(BF16)  12.7 us
  transfers between devices with their start and end apart: 73, of which 33 were waited for; matrix products, arithmetic and copies ran while one was open for 6% of the time, Pallas kernels for 27%

commit v1 on v0

--- a/solution.py
+++ b/solution.py
@@ -35,21 +35,22 @@
         "a dnown1 b a",
         "nback0 a aback0 nback1",
         "b a aback1 a",
-        "b late kv a",
-        "b fosib1 fosib0 kvpart",
+        "late b kv a",
+        "fosib1 fosib0 b kvpart",
         "a dn11 E b",
-        "e e b a",
-        "e input1 dn10 foown0",
-        "e a b e",
-        "input0 sums e a",
-        "b sums1 sums2 e",
-        "foown1 sums4 e b",
-        "out0 e sumscore a",
-        "e out1 sumschip b",
-        "e weave a b",
-        "a e sumsend putdown",
-        "e b putwide0 e",
-        "putlate b putwide1",
+        "e dn10 e b",
+        "a e input1 foown0",
+        "e a putdown0 b",
+        "e input0 sums sums1",
+        "e a b sums2",
+        "e foown1 e sums4",
+        "b out0 putwide0 e",
+        "a sumscore e out1",
+        "b sumschip e weave",
+        "a b a e",
+        "sumsend putdown1 e b",
+        "putwide1 putlate0 e putlate1",
+        "b putwide2",
     )
 ).split()
 
@@ -723,19 +724,40 @@
         )
         self.ring_b.begin(grad)
 
-    def putdown(self):
-        (self.down_sum,) = self.ring_a.assemble([shape((8, self.units // 8, self.width), F32)], 0, 8)
+    def put_down(self, first, last):
+        target = shape((8, self.units // 8, self.width), F32) if first == 0 else self.down_sum
+        (self.down_sum,) = self.ring_a.assemble([target], first, last)
+
+    def putdown0(self):
+        self.put_down(0, 4)
+
+    def putdown1(self):
+        self.put_down(4, 8)
+
+    def put_wide(self, first, last):
+        target = shape((2, 8, self.width // 8, self.units), F32) if first == 0 else self.gate_up_sum
+        (self.gate_up_sum,) = self.ring_b.assemble([target], first, last)
 
     def putwide0(self):
-        (self.gate_up_sum,) = self.ring_b.assemble([shape((2, 8, self.width // 8, self.units), F32)], 0, 6)
+        self.put_wide(0, 4)
 
     def putwide1(self):
-        (self.gate_up_sum,) = self.ring_b.assemble([self.gate_up_sum], 6, 8)
-
-    def putlate(self):
-        self.query_sum, self.out_sum = self.ring_e.assemble(
-            [shape((8, self.width // 8, self.cols), F32), shape((8, self.cols // 8, self.width), F32)], 0, 8
-        )
+        self.put_wide(4, 7)
+
+    def putwide2(self):
+        self.put_wide(7, 8)
+
+    def put_late(self, first, last):
+        targets = [shape((8, self.width // 8, self.cols), F32), shape((8, self.cols // 8, self.width), F32)]
+        if first:
+            targets = [self.query_sum, self.out_sum]
+        self.query_sum, self.out_sum = self.ring_e.assemble(targets, first, last)
+
+    def putlate0(self):
+        self.put_late(0, 6)
+
+    def putlate1(self):
+        self.put_late(6, 8)
 
     def rows_back(self, side, chunks, lefts, weight, dims, extra):
         rows, count = chunks * self.quarter, len(lefts) // chunks

time: 397 us -> 380 us (0.957)
  waiting for transfers between devices: 118 us -> 104 us
  starting transfers between devices: 105 us -> 97.6 us
  Pallas kernels: 121 us -> 126 us
  local copies, waits for them, and re-layouts: 23.4 us -> 27.4 us
    ppermute x42, waiting for transfers between devices: 88.8 us -> 71.5 us  [send(): self.arrived = lax.ppermute(self.travelling, ('dp', 'tensor'), ring_pairs())]
    ppermute x3, starting transfers between devices: 8.92 us -> 2.87 us  [over_dp(): lax.ppermute(field, 'dp', [(i, i ^ step) for i in range(n_dp)]).astype(F32)]
    pallas_call x14 -> x17, Pallas kernels: 60.7 us -> 65.8 us  [call(): pl.pallas_call(run, out_shape=outs + [shape((8, 128), F32)], grid_spec=pl...]
    unnamed x206 -> x196, local copies, waits for them, and re-layouts: 20.2 us -> 24.2 us
  transfers between devices with their start and end apart: 73 -> 73, of which waited for: 33 -> 34; matrix products, arithmetic and copies ran while one was open for 6% -> 5% of each run, Pallas kernels for 27% -> 30%
where the time goes in v1:
time: 380 us; the launch traced here: 373 us
  Pallas kernels  126 us (33%)
  waiting for transfers between devices  104 us (27%)
  starting transfers between devices  97.6 us (26%)
  local copies, waits for them, and re-layouts  27.4 us (7%)
  other arithmetic  15.5 us (4%)
    ppermute x42, starting transfers between devices, send(): self.arrived = lax.ppermute(self.travelling, ('dp', 'tensor'), ring_pairs())  76 us
    ppermute x42, waiting for transfers between devices, send(): self.arrived = lax.ppermute(self.travelling, ('dp', 'tensor'), ring_pairs())  71.5 us
    pallas_call x17, Pallas kernels, call(): pl.pallas_call(run, out_shape=outs + [shape((8, 128), F32)], grid_spec=pl...  65.8 us
    pallas_call x19, Pallas kernels, direct(): pl.pallas_call(run, out_shape=[pltpu.HBM(o.shape, o.dtype) if i in far el...  59.8 us
    unnamed x196, local copies, waits for them, and re-layouts  24.2 us
    ppermute x10, waiting for transfers between devices, swap_x(): return lax.ppermute(field, 'tensor', [(i, i ^ 2) for i in range(4)])  15.5 us
    ppermute x3, waiting for transfers between devices, over_dp(): lax.ppermute(field, 'dp', [(i, i ^ step) for i in range(n_dp)]).astype(F32)  13 us
    ppermute x10, starting transfers between devices, swap_x(): return lax.ppermute(field, 'tensor', [(i, i ^ 2) for i in range(4)])  12.5 us
  transfers between devices with their start and end apart: 73, of which 34 were waited for; matrix products, arithmetic and copies ran while one was open for 5% of the time, Pallas kernels for 30%

profile of v1, /device:TPU:0, one launch (start us, length us, event | category | flops | bytes accessed | tf_op | source)
XLA Modules:
  0.0 372.7 jit_solution(11109538286469071372)
XLA Ops:
  1.9 5.1 %shard_map.169 = (bf16[960,128]{1,0:T(8,128)(2,1)S(1)}, bf16[960,128]{1,0:T(8,128)(2,1)S(1)}, bf16[240,1536]{1,0:T(8,128)(2,1)S(1)}, bf16[240,1536]{1,0:T(8,128)...) custom-call(s32[1]{0:T(128)} %bitcast.refs_0_, ...), custom_call_target="tpu_custom_call" | custom-call | tf_op jit(solution)/shard_map/pallas_call | solution.py:122
  8.6 7.9 %shard_map.170 = (bf16[240,1536]{1,0:T(8,128)(2,1)S(1)}, bf16[240,768]{1,0:T(8,128)(2,1)}, bf16[240,768]{1,0:T(8,128)(2,1)}, f32[240,8]{1,0:T(8,128)}, bf16[240,...) custom-call(s32[1]{0:T(128)} %bitcast.refs_0_, s32[4]{0:T(128)S(1)} %add_add_fusion.1.refs_1_, ...), custom_call_target="tpu_custom_call" | custom-call | tf_op jit(solution)/shard_map/pallas_call | solution.py:96
  19.5 9.6 %shard_map.171 = (bf16[240,1536]{1,0:T(8,128)(2,1)S(1)}, bf16[240,768]{1,0:T(8,128)(2,1)}, bf16[240,768]{1,0:T(8,128)(2,1)}, f32[240,8]{1,0:T(8,128)}, bf16[240,...) custom-call(s32[1]{0:T(128)} %bitcast.1.refs_0_, ...), custom_call_target="tpu_custom_call" | custom-call | tf_op jit(solution)/shard_map/pallas_call | solution.py:96
  33.1 3.7 collective-permute-done.2.refs_3_
  43.0 4.1 %shard_map.175 = (bf16[480,1152]{1,0:T(8,128)(2,1)S(1)}, bf16[480,1152]{1,0:T(8,128)(2,1)S(1)}, bf16[480,1152]{1,0:T(8,128)(2,1)S(1)}, bf16[480,1536]{1,0:T(8,128)(2,1)S(1)}, f32[8,128]{1,0:T(8,128)S(1)}) custom-call(bf16[128,1536]{1,0:T(8,128)(2,1)S(1)} %get-tuple-element.293.refs_0_, bf16[112,1536]{1,0:T(8,128)(2,1)S(1)} %get-tuple-element.294.refs_1_, ...), custom_call_target="tpu_custom_call" | custom-call | tf_op jit(solution)/shard_map/pallas_call | solution.py:122
  63.8 5.9 %shard_map.178 = (bf16[480,1152]{1,0:T(8,128)(2,1)S(1)}, bf16[480,1152]{1,0:T(8,128)(2,1)S(1)}, bf16[480,1152]{1,0:T(8,128)(2,1)S(1)}, bf16[480,1536]{1,0:T(8,128)(2,1)S(1)}, f32[8,128]{1,0:T(8,128)S(1)}) custom-call(bf16[128,1536]{1,0:T(8,128)(2,1)} %get-tuple-element.306.refs_0_, bf16[112,1536]{1,0:T(8,128)(2,1)} %get-tuple-element.307.refs_1_, ...), custom_call_target="tpu_custom_call" | custom-call | tf_op jit(solution)/shard_map/pallas_call | solution.py:122
  69.8 9.1 %shard_map.179 = (bf16[8,192,2304]{2,1,0:T(8,128)(2,1)S(1)}, f32[8,128]{1,0:T(8,128)S(1)}) custom-call(s32[2]{0:T(128)S(1)} %pad_add_fusion.refs_0_, bf16[480,1536]{1,0:T(8,128)(2,1)S(1)} %copy-done.37, bf16[480,1536]{1,0:T(8,128)(2,1)S(1)} %get-tuple-element.313.refs_2_, bf16[480,1152]{1,0:T(8,128)(2,1)S(1)} %copy-done.21, ...), custom_call_target="tpu_custom_call" | custom-call | tf_op jit(solution)/shard_map/pallas_call | solution.py:122
  83.8 4.5 %shard_map.181 = (bf16[8,144,1536]{2,1,0:T(8,128)(2,1)S(1)}, f32[8,128]{1,0:T(8,128)S(1)}) custom-call(s32[2]{0:T(128)S(1)} %pad_add_fusion.refs_0_, bf16[480,1152]{1,0:T(8,128)(2,1)S(1)} %copy-done.18, bf16[480,1152]{1,0:T(8,128)(2,1)S(1)} %get-tuple-element.310.refs_2_.refs_0_, bf16[480,1536]{1,0:T(8,128)(2,1)S(1)} %copy-done.14, ...), custom_call_target="tpu_custom_call" | custom-call | tf_op jit(solution)/shard_map/pallas_call | solution.py:122
  92.7 4.5 %collective-permute-done.9 = bf16[144,1536]{1,0:T(8,128)(2,1)S(1)} collective-permute-done((bf16[144,1536]{1,0:T(8,128)(2,1)S(1)}, bf16[144,1536]{1,0:T(8,128)(2,1)S(1)}, u32[]{:S(2)}, u32[]{:S(2)}) %collective-permute-start.9) | collective-permute-done | bytes 442400 | tf_op jit(solution)/shard_map/ppermute | solution.py:513
  110.2 4.9 %collective-permute-done.13 = bf16[192,2304]{1,0:T(8,128)(2,1)S(1)} collective-permute-done((bf16[192,2304]{1,0:T(8,128)(2,1)S(1)}, bf16[192,2304]{1,0:T(8,128)(2,1)S(1)}, u32[]{:S(2)}, u32[]{:S(2)}) %collective-permute-start.13) | collective-permute-done | bytes 884768 | tf_op jit(solution)/shard_map/ppermute | solution.py:513
  115.4 4.5 %collective-permute-done.12 = bf16[144,1536]{1,0:T(8,128)(2,1)S(1)} collective-permute-done((bf16[144,1536]{1,0:T(8,128)(2,1)S(1)}, bf16[144,1536]{1,0:T(8,128)(2,1)S(1)}, u32[]{:S(2)}, u32[]{:S(2)}) %collective-permute-start.12) | collective-permute-done | bytes 442400 | tf_op jit(solution)/shard_map/ppermute | solution.py:513
  130.6 3.5 shard_map.185
  134.1 5.8 %collective-permute-done.19.refs_2_ = bf16[240,1536]{1,0:T(8,128)(2,1)S(1)} collective-permute-done((bf16[240,1536]{1,0:T(8,128)(2,1)S(1)}, bf16[240,1536]{1,0:T(8,128)(2,1)S(1)}, u32[]{:S(2)}, u32[]{:S(2)}) %collective-permute-start.19) | collective-permute-done | bytes 737312 | tf_op jit(solution)/shard_map/ppermute | solution.py:67
  146.5 6.0 %shard_map.187 = (bf16[240,768]{1,0:T(8,128)(2,1)S(1)}, f32[480,256]{1,0:T(8,128)S(1)}, bf16[480,256]{1,0:T(8,128)(2,1)S(1)}, f32[8,128]{1,0:T(8,128)S(1)}) custom-call(s32[1]{0:T(128)} %bitcast.refs_0_, bf16[240,768]{1,0:T(8,128)(2,1)S(1)} %copy-done.65, f32[240,8]{1,0:T(8,128)S(1)} %copy-done.77, bf16[240,768]{1,0:T(8,128)(2,1)S(1)} %get-tuple-element.368.refs_3_, ...), custom_call_target="tpu_custom_call" | custom-call | tf_op jit(solution)/shard_map/pallas_call | solution.py:96
  154.2 3.7 shard_map.188
  171.6 3.4 collective-permute-done.27
  178.7 4.7 %collective-permute-done.26 = bf16[480,256]{1,0:T(8,128)(2,1)S(1)} collective-permute-done((bf16[480,256]{1,0:T(8,128)(2,1)S(1)}, bf16[480,256]{1,0:T(8,128)(2,1)S(1)}, u32[]{:S(2)}, u32[]{:S(2)}) %collective-permute-start.26) | collective-permute-done | bytes 245792 | tf_op jit(solution)/shard_map/ppermute | solution.py:67
  213.4 3.2 collective-permute-done.33
  231.8 4.1 %shard_map.195 = (f32[8,144,1536]{2,1,0:T(8,128)}, f32[8,128]{1,0:T(8,128)S(1)}) custom-call(s32[2]{0:T(128)S(1)} %copy-done.80, bf16[144,1536]{1,0:T(8,128)(2,1)S(1)} %copy-done.35, bf16[144,1536]{1,0:T(8,128)(2,1)} %collective-permute-done.25.refs_2_, bf16[144,1536]{1,0:T(8,128)(2,1)S(1)} %collective-permute-done.34.refs_3_, ...), custom_call_target="tpu_custom_call" | custom-call | tf_op jit(solution)/shard_map/pallas_call | solution.py:96
  246.0 3.3 shard_map.196
  253.8 7.8 %collective-permute-done.40.refs_3_ = bf16[192,2304]{1,0:T(8,128)(2,1)} collective-permute-done((bf16[192,2304]{1,0:T(8,128)(2,1)}, bf16[192,2304]{1,0:T(8,128)(2,1)}, u32[]{:S(2)}, u32[]{:S(2)}) %collective-permute-start.40) | collective-permute-done | bytes 884768 | tf_op jit(solution)/shard_map/ppermute | solution.py:513
  272.9 3.8 %collective-permute-done.48 = bf16[792,128]{1,0:T(8,128)(2,1)S(1)} collective-permute-done((bf16[792,128]{1,0:T(8,128)(2,1)S(1)}, bf16[792,128]{1,0:T(8,128)(2,1)S(1)}, u32[]{:S(2)}, u32[]{:S(2)}) %collective-permute-start.48) | collective-permute-done | bytes 202784 | tf_op jit(solution)/shard_map/ppermute | solution.py:560
  276.8 3.1 collective-permute-done.50.refs_2_
  284.8 7.1 %collective-permute-done.55 = bf16[792,128]{1,0:T(8,128)(2,1)S(1)} collective-permute-done((bf16[792,128]{1,0:T(8,128)(2,1)S(1)}, bf16[792,128]{1,0:T(8,128)(2,1)S(1)}, u32[]{:S(2)}, u32[]{:S(2)}) %collective-permute-start.55) | collective-permute-done | bytes 202784 | tf_op jit(solution)/shard_map/ppermute | solution.py:560
  292.7 5.3 %shard_map.198 = (f32[2,8,192,1152]{3,2,1,0:T(8,128)}, f32[8,128]{1,0:T(8,128)S(1)}) custom-call(s32[2]{0:T(128)S(1)} %copy-done.80, bf16[192,2304]{1,0:T(8,128)(2,1)S(1)} %copy-done.33, bf16[192,2304]{1,0:T(8,128)(2,1)} %collective-permute-done.37.refs_2_, bf16[192,2304]{1,0:T(8,128)(2,1)} %collective-permute-done.40.refs_3_, ...), custom_call_target="tpu_custom_call" | custom-call | tf_op jit(solution)/shard_map/pallas_call | solution.py:96
  300.2 4.2 %collective-permute-start.54 = (bf16[192,768]{1,0:T(8,128)(2,1)S(1)}, bf16[192,768]{1,0:T(8,128)(2,1)S(1)}, u32[]{:S(2)}, u32[]{:S(2)}) collective-permute-start(bf16[192,768]{1,0:T(8,128)(2,1)S(1)} %collective-permute-done.53.refs_3_), channel_id=1, source_target_pairs={{0,8},{8,16},{16,24},{24,28},{28,20},{20,12},{12,4},{4,0},{5,13},{... | collective-permute-start | bytes 884744 | tf_op jit(solution)/shard_map/ppermute | solution.py:513
  324.0 4.0 %shard_map.199 = (bf16[960,1536]{1,0:T(8,128)(2,1)}, bf16[960,1536]{1,0:T(8,128)(2,1)}, f32[8,128]{1,0:T(8,128)S(1)}) custom-call(s32[4]{0:T(128)S(1)} %add_add_fusion.refs_0_, bf16[240,1536]{1,0:T(8,128)(2,1)S(1)} %add_convert_fusion.2.refs_1_, bf16[240,1536]{1,0:T(8,128)(2,1)S(1)} %add_convert_fusion.1.refs_2_, ...), custom_call_target="tpu_custom_call" | custom-call | tf_op jit(solution)/shard_map/pallas_call | solution.py:122
  327.9 3.5 collective-permute-done.65.refs_3_
  343.9 3.9 %shard_map.200 = (f32[8,144,1536]{2,1,0:T(8,128)}, f32[8,128]{1,0:T(8,128)S(1)}) custom-call(s32[2]{0:T(128)S(1)} %copy-done.80, bf16[144,1536]{1,0:T(8,128)(2,1)} %collective-permute-done.41.refs_1_, bf16[144,1536]{1,0:T(8,128)(2,1)S(1)} %copy-done.64, bf16[144,1536]{1,0:T(8,128)(2,1)S(1)} %collective-permute-done.65.refs_3_, ...), custom_call_target="tpu_custom_call", output_to_operand_aliasing={{0}: (5, {})} | custom-call | tf_op jit(solution)/shard_map/pallas_call | solution.py:96
  347.9 4.4 %collective-permute-done.68.refs_1_ = bf16[192,768]{1,0:T(8,128)(2,1)S(1)} collective-permute-done((bf16[192,768]{1,0:T(8,128)(2,1)S(1)}, bf16[192,768]{1,0:T(8,128)(2,1)S(1)}, u32[]{:S(2)}, u32[]{:S(2)}) %collective-permute-start.68) | collective-permute-done | bytes 294944 | tf_op jit(solution)/shard_map/ppermute | solution.py:513
  358.3 4.8 %shard_map.201 = (f32[2,8,192,1152]{3,2,1,0:T(8,128)}, f32[8,128]{1,0:T(8,128)S(1)}) custom-call(s32[2]{0:T(128)S(1)} %copy-done.80, bf16[192,2304]{1,0:T(8,128)(2,1)} %collective-permute-done.63.refs_1_, bf16[192,2304]{1,0:T(8,128)(2,1)} %collective-permute-done.67.refs_2_, ...), custom_call_target="tpu_custom_call", output_to_operand_aliasing={{0}: (4, {})} | custom-call | tf_op jit(solution)/shard_map/pallas_call | solution.py:96
  363.1 3.4 shard_map.202
  (400 shorter events, 213.6 us)
Async XLA Ops:
  16.6 20.2 %collective-permute-start.2 = (bf16[240,1536]{1,0:T(8,128)(2,1)S(1)}, bf16[240,1536]{1,0:T(8,128)(2,1)S(1)}, u32[]{:S(2)}, u32[]{:S(2)}) collective-permute-start(bf16[240,1536]{1,0:T(8,128)(2,1)S(1)} %get-tuple-element.284.refs_2_), channel_id=1, source_target_pairs={{0,2},{1,3},{2,0},{3,1},{4,6},{5,7},{6,4},{7,5},{8,10},{9,11},{10,... | collective-permute-start | bytes 2211848 | tf_op jit(solution)/shard_map/ppermute | solution.py:67
  29.2 23.2 %collective-permute-start.5 = (bf16[240,1536]{1,0:T(8,128)(2,1)S(1)}, bf16[240,1536]{1,0:T(8,128)(2,1)S(1)}, u32[]{:S(2)}, u32[]{:S(2)}) collective-permute-start(bf16[240,1536]{1,0:T(8,128)(2,1)S(1)} %get-tuple-element.301.refs_2_), channel_id=1, source_target_pairs={{0,2},{1,3},{2,0},{3,1},{4,6},{5,7},{6,4},{7,5},{8,10},{9,11},{10,... | collective-permute-start | bytes 2211848 | tf_op jit(solution)/shard_map/ppermute | solution.py:67
  56.9 24.6 %collective-permute-start.8 = (bf16[240,1536]{1,0:T(8,128)(2,1)}, bf16[240,1536]{1,0:T(8,128)(2,1)S(1)}, u32[]{:S(2)}, u32[]{:S(2)}) collective-permute-start(bf16[240,1536]{1,0:T(8,128)(2,1)} %copy-done.88), channel_id=1, source_target_pairs={{0,1},{1,0},{2,3},{3,2},{4,5},{5,4},{6,7},{7,6},{8,9},{9,8},{10,11... | collective-permute-start | bytes 2211848 | tf_op jit(solution)/shard_map/ppermute | solution.py:63
  99.4 15.7 %collective-permute-start.13 = (bf16[192,2304]{1,0:T(8,128)(2,1)S(1)}, bf16[192,2304]{1,0:T(8,128)(2,1)S(1)}, u32[]{:S(2)}, u32[]{:S(2)}) collective-permute-start(bf16[192,2304]{1,0:T(8,128)(2,1)S(1)} %fusion.6), channel_id=1, source_target_pairs={{0,8},{8,16},{16,24},{24,28},{28,20},{20,12},{12,4},{4,0},{5,13},{... | collective-permute-start | bytes 2654216 | tf_op jit(solution)/shard_map/ppermute | solution.py:513
  103.4 21.8 %collective-permute-start.16 = (bf16[240,1536]{1,0:T(8,128)(2,1)S(1)}, bf16[240,1536]{1,0:T(8,128)(2,1)S(1)}, u32[]{:S(2)}, u32[]{:S(2)}) collective-permute-start(bf16[240,1536]{1,0:T(8,128)(2,1)S(1)} %get-tuple-element.343.refs_1_), channel_id=1, source_target_pairs={{0,2},{1,3},{2,0},{3,1},{4,6},{5,7},{6,4},{7,5},{8,10},{9,11},{10,... | collective-permute-start | bytes 2211848 | tf_op jit(solution)/shard_map/ppermute | solution.py:67
  105.8 14.1 %collective-permute-start.12 = (bf16[144,1536]{1,0:T(8,128)(2,1)S(1)}, bf16[144,1536]{1,0:T(8,128)(2,1)S(1)}, u32[]{:S(2)}, u32[]{:S(2)}) collective-permute-start(bf16[144,1536]{1,0:T(8,128)(2,1)S(1)} %fusion.16), channel_id=1, source_target_pairs={{0,8},{8,16},{16,24},{24,28},{28,20},{20,12},{12,4},{4,0},{5,13},{... | collective-permute-start | bytes 1327112 | tf_op jit(solution)/shard_map/ppermute | solution.py:513
  122.1 20.3 %collective-permute-start.18 = (bf16[192,2304]{1,0:T(8,128)(2,1)S(1)}, bf16[192,2304]{1,0:T(8,128)(2,1)S(1)}, u32[]{:S(2)}, u32[]{:S(2)}) collective-permute-start(bf16[192,2304]{1,0:T(8,128)(2,1)S(1)} %fusion.5), channel_id=1, source_target_pairs={{0,8},{8,16},{16,24},{24,28},{28,20},{20,12},{12,4},{4,0},{5,13},{... | collective-permute-start | bytes 2654216 | tf_op jit(solution)/shard_map/ppermute | solution.py:513
  123.7 16.2 %collective-permute-start.19 = (bf16[240,1536]{1,0:T(8,128)(2,1)S(1)}, bf16[240,1536]{1,0:T(8,128)(2,1)S(1)}, u32[]{:S(2)}, u32[]{:S(2)}) collective-permute-start(bf16[240,1536]{1,0:T(8,128)(2,1)S(1)} %get-tuple-element.351.refs_1_), channel_id=1, source_target_pairs={{0,2},{1,3},{2,0},{3,1},{4,6},{5,7},{6,4},{7,5},{8,10},{9,11},{10,... | collective-permute-start | bytes 2211848 | tf_op jit(solution)/shard_map/ppermute | solution.py:67
  128.4 14.2 %collective-permute-start.17 = (bf16[144,1536]{1,0:T(8,128)(2,1)S(1)}, bf16[144,1536]{1,0:T(8,128)(2,1)S(1)}, u32[]{:S(2)}, u32[]{:S(2)}) collective-permute-start(bf16[144,1536]{1,0:T(8,128)(2,1)S(1)} %fusion.14), channel_id=1, source_target_pairs={{0,8},{8,16},{16,24},{24,28},{28,20},{20,12},{12,4},{4,0},{5,13},{... | collective-permute-start | bytes 1327112 | tf_op jit(solution)/shard_map/ppermute | solution.py:513
  144.8 15.9 %collective-permute-start.23 = (bf16[192,2304]{1,0:T(8,128)(2,1)S(1)}, bf16[192,2304]{1,0:T(8,128)(2,1)S(1)}, u32[]{:S(2)}, u32[]{:S(2)}) collective-permute-start(bf16[192,2304]{1,0:T(8,128)(2,1)S(1)} %fusion.4), channel_id=1, source_target_pairs={{0,8},{8,16},{16,24},{24,28},{28,20},{20,12},{12,4},{4,0},{5,13},{... | collective-permute-start | bytes 2654216 | tf_op jit(solution)/shard_map/ppermute | solution.py:513
  157.9 27.9 %collective-permute-start.29 = (bf16[8,192,768]{2,1,0:T(8,128)(2,1)S(1)}, bf16[8,192,768]{2,1,0:T(8,128)(2,1)S(1)}, u32[]{:S(2)}, u32[]{:S(2)}) collective-permute-start(bf16[8,192,768]{2,1,0:T(8,128)(2,1)S(1)} %get-tuple-element.413), channel_id=1, source_target_pairs={{0,1},{1,0},{2,3},{3,2},{4,5},{5,4},{6,7},{7,6},{8,9},{9,8},{10,11... | collective-permute-start | bytes 7077896 | tf_op jit(solution)/shard_map/ppermute | solution.py:63
  192.2 19.5 %collective-permute-start.35 = (bf16[192,2304]{1,0:T(8,128)(2,1)}, bf16[192,2304]{1,0:T(8,128)(2,1)}, u32[]{:S(2)}, u32[]{:S(2)}) collective-permute-start(bf16[192,2304]{1,0:T(8,128)(2,1)} %fusion.1), channel_id=1, source_target_pairs={{0,8},{8,16},{16,24},{24,28},{28,20},{20,12},{12,4},{4,0},{5,13},{... | collective-permute-start | bytes 2654216 | tf_op jit(solution)/shard_map/ppermute | solution.py:513
  198.7 26.5 %collective-permute-start.24 = (bf16[240,1536]{1,0:T(8,128)(2,1)}, bf16[240,1536]{1,0:T(8,128)(2,1)S(1)}, u32[]{:S(2)}, u32[]{:S(2)}) collective-permute-start(bf16[240,1536]{1,0:T(8,128)(2,1)} %copy-done.87), channel_id=1, source_target_pairs={{0,1},{1,0},{2,3},{3,2},{4,5},{5,4},{6,7},{7,6},{8,9},{9,8},{10,11... | collective-permute-start | bytes 2211848 | tf_op jit(solution)/shard_map/ppermute | solution.py:63
  198.7 14.7 %collective-permute-start.34 = (bf16[144,1536]{1,0:T(8,128)(2,1)}, bf16[144,1536]{1,0:T(8,128)(2,1)S(1)}, u32[]{:S(2)}, u32[]{:S(2)}) collective-permute-start(bf16[144,1536]{1,0:T(8,128)(2,1)} %collective-permute-done.25.refs_2_), channel_id=1, source_target_pairs={{0,8},{8,16},{16,24},{24,28},{28,20},{20,12},{12,4},{4,0},{5,13},{... | collective-permute-start | bytes 1327112 | tf_op jit(solution)/shard_map/ppermute | solution.py:513
  200.5 20.5 %collective-permute-start.28 = (bf16[240,1536]{1,0:T(8,128)(2,1)}, bf16[240,1536]{1,0:T(8,128)(2,1)S(1)}, u32[]{:S(2)}, u32[]{:S(2)}) collective-permute-start(bf16[240,1536]{1,0:T(8,128)(2,1)} %copy-done.57), channel_id=1, source_target_pairs={{0,2},{1,3},{2,0},{3,1},{4,6},{5,7},{6,4},{7,5},{8,10},{9,11},{10,... | collective-permute-start | bytes 2211848 | tf_op jit(solution)/shard_map/ppermute | solution.py:67
  219.5 26.5 %collective-permute-start.45 = (bf16[240,1536]{1,0:T(8,128)(2,1)S(1)}, bf16[240,1536]{1,0:T(8,128)(2,1)S(1)}, u32[]{:S(2)}, u32[]{:S(2)}) collective-permute-start(bf16[240,1536]{1,0:T(8,128)(2,1)S(1)} %get-tuple-element.457.refs_2_), channel_id=1, source_target_pairs={{0,2},{1,3},{2,0},{3,1},{4,6},{5,7},{6,4},{7,5},{8,10},{9,11},{10,... | collective-permute-start | bytes 2211848 | tf_op jit(solution)/shard_map/ppermute | solution.py:67
  230.5 40.1 %collective-permute-start.51 = (bf16[240,1536]{1,0:T(8,128)(2,1)}, bf16[240,1536]{1,0:T(8,128)(2,1)}, u32[]{:S(2)}, u32[]{:S(2)}) collective-permute-start(bf16[240,1536]{1,0:T(8,128)(2,1)} %get-tuple-element.479), channel_id=1, source_target_pairs={{0,1},{1,0},{2,3},{3,2},{4,5},{5,4},{6,7},{7,6},{8,9},{9,8},{10,11... | collective-permute-start | bytes 2211848 | tf_op jit(solution)/shard_map/ppermute | solution.py:63
  231.3 22.4 %collective-permute-start.41 = (bf16[144,1536]{1,0:T(8,128)(2,1)}, bf16[144,1536]{1,0:T(8,128)(2,1)}, u32[]{:S(2)}, u32[]{:S(2)}) collective-permute-start(bf16[144,1536]{1,0:T(8,128)(2,1)} %collective-permute-done.38.refs_4_), channel_id=1, source_target_pairs={{0,8},{8,16},{16,24},{24,28},{28,20},{20,12},{12,4},{4,0},{5,13},{... | collective-permute-start | bytes 1327112 | tf_op jit(solution)/shard_map/ppermute | solution.py:513
  244.3 17.3 %collective-permute-start.40 = (bf16[192,2304]{1,0:T(8,128)(2,1)}, bf16[192,2304]{1,0:T(8,128)(2,1)}, u32[]{:S(2)}, u32[]{:S(2)}) collective-permute-start(bf16[192,2304]{1,0:T(8,128)(2,1)} %collective-permute-done.37.refs_2_), channel_id=1, source_target_pairs={{0,8},{8,16},{16,24},{24,28},{28,20},{20,12},{12,4},{4,0},{5,13},{... | collective-permute-start | bytes 2654216 | tf_op jit(solution)/shard_map/ppermute | solution.py:513
  252.6 14.2 %collective-permute-start.49 = (bf16[192,768]{1,0:T(8,128)(2,1)S(1)}, bf16[192,768]{1,0:T(8,128)(2,1)S(1)}, u32[]{:S(2)}, u32[]{:S(2)}) collective-permute-start(bf16[192,768]{1,0:T(8,128)(2,1)S(1)} %fusion.19), channel_id=1, source_target_pairs={{0,8},{8,16},{16,24},{24,28},{28,20},{20,12},{12,4},{4,0},{5,13},{... | collective-permute-start | bytes 884744 | tf_op jit(solution)/shard_map/ppermute | solution.py:513
  261.6 20.7 %collective-permute-start.46 = (bf16[192,2304]{1,0:T(8,128)(2,1)}, bf16[192,2304]{1,0:T(8,128)(2,1)S(1)}, u32[]{:S(2)}, u32[]{:S(2)}) collective-permute-start(bf16[192,2304]{1,0:T(8,128)(2,1)} %collective-permute-done.40.refs_3_), channel_id=1, source_target_pairs={{0,8},{8,16},{16,24},{24,28},{28,20},{20,12},{12,4},{4,0},{5,13},{... | collective-permute-start | bytes 2654216 | tf_op jit(solution)/shard_map/ppermute | solution.py:513
  270.0 22.7 %collective-permute-start.36 = (bf16[240,1536]{1,0:T(8,128)(2,1)S(1)}, bf16[240,1536]{1,0:T(8,128)(2,1)S(1)}, u32[]{:S(2)}, u32[]{:S(2)}) collective-permute-start(bf16[240,1536]{1,0:T(8,128)(2,1)S(1)} %copy-done.49), channel_id=1, source_target_pairs={{0,2},{1,3},{2,0},{3,1},{4,6},{5,7},{6,4},{7,5},{8,10},{9,11},{10,... | collective-permute-start | bytes 2211848 | tf_op jit(solution)/shard_map/ppermute | solution.py:67
  282.3 30.5 %collective-permute-start.63 = (bf16[192,2304]{1,0:T(8,128)(2,1)S(1)}, bf16[192,2304]{1,0:T(8,128)(2,1)}, u32[]{:S(2)}, u32[]{:S(2)}) collective-permute-start(bf16[192,2304]{1,0:T(8,128)(2,1)S(1)} %collective-permute-done.46.refs_4_), channel_id=1, source_target_pairs={{0,8},{8,16},{16,24},{24,28},{28,20},{20,12},{12,4},{4,0},{5,13},{... | collective-permute-start | bytes 2654216 | tf_op jit(solution)/shard_map/ppermute | solution.py:513
  284.8 15.5 %collective-permute-start.53 = (bf16[192,768]{1,0:T(8,128)(2,1)S(1)}, bf16[192,768]{1,0:T(8,128)(2,1)S(1)}, u32[]{:S(2)}, u32[]{:S(2)}) collective-permute-start(bf16[192,768]{1,0:T(8,128)(2,1)S(1)} %collective-permute-done.50.refs_2_), channel_id=1, source_target_pairs={{0,8},{8,16},{16,24},{24,28},{28,20},{20,12},{12,4},{4,0},{5,13},{... | collective-permute-start | bytes 884744 | tf_op jit(solution)/shard_map/ppermute | solution.py:513
  284.8 30.4 %collective-permute-start.60 = (bf16[240,1536]{1,0:T(8,128)(2,1)S(1)}, bf16[240,1536]{1,0:T(8,128)(2,1)S(1)}, u32[]{:S(2)}, u32[]{:S(2)}) collective-permute-start(bf16[240,1536]{1,0:T(8,128)(2,1)S(1)} %copy-done.55), channel_id=1, source_target_pairs={{0,1},{1,0},{2,3},{3,2},{4,5},{5,4},{6,7},{7,6},{8,9},{9,8},{10,11... | collective-permute-start | bytes 2211848 | tf_op jit(solution)/shard_map/ppermute | solution.py:63
  291.9 18.4 %collective-permute-start.52 = (bf16[240,1536]{1,0:T(8,128)(2,1)S(1)}, bf16[240,1536]{1,0:T(8,128)(2,1)S(1)}, u32[]{:S(2)}, u32[]{:S(2)}) collective-permute-start(bf16[240,1536]{1,0:T(8,128)(2,1)S(1)} %get-tuple-element.499), channel_id=1, source_target_pairs={{0,2},{1,3},{2,0},{3,1},{4,6},{5,7},{6,4},{7,5},{8,10},{9,11},{10,... | collective-permute-start | bytes 2211848 | tf_op jit(solution)/shard_map/ppermute | solution.py:67
  305.1 15.7 %collective-permute-start.59 = (bf16[240,1536]{1,0:T(8,128)(2,1)}, bf16[240,1536]{1,0:T(8,128)(2,1)}, u32[]{:S(2)}, u32[]{:S(2)}) collective-permute-start(bf16[240,1536]{1,0:T(8,128)(2,1)} %get-tuple-element.501.refs_5_), channel_id=1, source_target_pairs={{0,1},{1,0},{2,3},{3,2},{4,5},{5,4},{6,7},{7,6},{8,9},{9,8},{10,11... | collective-permute-start | bytes 2211848 | tf_op jit(solution)/shard_map/ppermute | solution.py:63
  312.8 20.9 %collective-permute-start.67 = (bf16[192,2304]{1,0:T(8,128)(2,1)}, bf16[192,2304]{1,0:T(8,128)(2,1)}, u32[]{:S(2)}, u32[]{:S(2)}) collective-permute-start(bf16[192,2304]{1,0:T(8,128)(2,1)} %collective-permute-done.63.refs_1_), channel_id=1, source_target_pairs={{0,8},{8,16},{16,24},{24,28},{28,20},{20,12},{12,4},{4,0},{5,13},{... | collective-permute-start | bytes 2654216 | tf_op jit(solution)/shard_map/ppermute | solution.py:513
  317.3 14.1 %collective-permute-start.65 = (bf16[144,1536]{1,0:T(8,128)(2,1)}, bf16[144,1536]{1,0:T(8,128)(2,1)S(1)}, u32[]{:S(2)}, u32[]{:S(2)}) collective-permute-start(bf16[144,1536]{1,0:T(8,128)(2,1)} %copy-done.63), channel_id=1, source_target_pairs={{0,8},{8,16},{16,24},{24,28},{28,20},{20,12},{12,4},{4,0},{5,13},{... | collective-permute-start | bytes 1327112 | tf_op jit(solution)/shard_map/ppermute | solution.py:513
  320.7 18.9 %collective-permute-start.64 = (bf16[192,768]{1,0:T(8,128)(2,1)}, bf16[192,768]{1,0:T(8,128)(2,1)S(1)}, u32[]{:S(2)}, u32[]{:S(2)}) collective-permute-start(bf16[192,768]{1,0:T(8,128)(2,1)} %copy-done.75), channel_id=1, source_target_pairs={{0,8},{8,16},{16,24},{24,28},{28,20},{20,12},{12,4},{4,0},{5,13},{... | collective-permute-start | bytes 884744 | tf_op jit(solution)/shard_map/ppermute | solution.py:513
  333.8 18.6 %collective-permute-start.71 = (bf16[192,2304]{1,0:T(8,128)(2,1)}, bf16[192,2304]{1,0:T(8,128)(2,1)S(1)}, u32[]{:S(2)}, u32[]{:S(2)}) collective-permute-start(bf16[192,2304]{1,0:T(8,128)(2,1)} %collective-permute-done.67.refs_2_), channel_id=1, source_target_pairs={{0,8},{8,16},{16,24},{24,28},{28,20},{20,12},{12,4},{4,0},{5,13},{... | collective-permute-start | bytes 2654216 | tf_op jit(solution)/shard_map/ppermute | solution.py:513
  352.3 17.9 %collective-permute-start.72 = (bf16[192,2304]{1,0:T(8,128)(2,1)S(1)}, bf16[192,2304]{1,0:T(8,128)(2,1)S(1)}, u32[]{:S(2)}, u32[]{:S(2)}) collective-permute-start(bf16[192,2304]{1,0:T(8,128)(2,1)S(1)} %collective-permute-done.71.refs_3_), channel_id=1, source_target_pairs={{0,8},{8,16},{16,24},{24,28},{28,20},{20,12},{12,4},{4,0},{5,13},{... | collective-permute-start | bytes 2654216 | tf_op jit(solution)/shard_map/ppermute | solution.py:513
  (139 other events, 1273.9 us)

commit v2 on v1

--- a/solution.py
+++ b/solution.py
@@ -858,7 +858,7 @@
     def late(self):
         self.late_mine, other = self.chain.direct(
             functools.partial(late_grad_kernel, self.cols),
-            [shape((8, self.width // 8, 2 * self.cols), t) for t in (F32, BF16)],
+            [shape((8, self.width // 8, 2 * self.cols), BF16)] * 2,
             [
                 *self.far_normed1, *self.d_queries, self.head_out0, self.head_out1, self.d_res_low0, self.d_res_low1,
             ],
@@ -993,7 +993,7 @@
         self.kv_out = jnp.concatenate([columns[0], columns[1]], 1).astype(F32)
 
     def E(self):
-        (grad,) = self.chain.after((self.late_mine + self.late_from.astype(F32)).astype(BF16))
+        (grad,) = self.chain.after((self.late_mine.astype(F32) + self.late_from.astype(F32)).astype(BF16))
         self.ring_e.begin(grad)
 
     def e(self):

time: 380 us -> 380 us (level)
    unnamed x196 -> x200, local copies, waits for them, and re-layouts: 24.2 us -> 24.4 us
  transfers between devices with their start and end apart: 73 -> 73, of which waited for: 34 -> 35; matrix products, arithmetic and copies ran while one was open for 5% -> 5% of each run, Pallas kernels for 30% -> 30%
where the time goes in v2:
time: 380 us; the launch traced here: 373 us
  Pallas kernels  125 us (33%)
  waiting for transfers between devices  107 us (28%)
  starting transfers between devices  94.7 us (25%)
  local copies, waits for them, and re-layouts  27.6 us (7%)
  other arithmetic  15.4 us (4%)
    ppermute x42, waiting for transfers between devices, send(): self.arrived = lax.ppermute(self.travelling, ('dp', 'tensor'), ring_pairs())  74.8 us
    ppermute x42, starting transfers between devices, send(): self.arrived = lax.ppermute(self.travelling, ('dp', 'tensor'), ring_pairs())  73 us
    pallas_call x17, Pallas kernels, call(): pl.pallas_call(run, out_shape=outs + [shape((8, 128), F32)], grid_spec=pl...  65.6 us
    pallas_call x19, Pallas kernels, direct(): pl.pallas_call(run, out_shape=[pltpu.HBM(o.shape, o.dtype) if i in far el...  59.7 us
    unnamed x200, local copies, waits for them, and re-layouts  24.4 us
    ppermute x10, waiting for transfers between devices, swap_x(): return lax.ppermute(field, 'tensor', [(i, i ^ 2) for i in range(4)])  15.6 us
    ppermute x3, waiting for transfers between devices, over_dp(): lax.ppermute(field, 'dp', [(i, i ^ step) for i in range(n_dp)]).astype(F32)  12.9 us
    ppermute x10, starting transfers between devices, swap_x(): return lax.ppermute(field, 'tensor', [(i, i ^ 2) for i in range(4)])  12.6 us
  transfers between devices with their start and end apart: 73, of which 35 were waited for; matrix products, arithmetic and copies ran while one was open for 5% of the time, Pallas kernels for 30%

profile of v2, /device:TPU:0, one launch (start us, length us, event | category | flops | bytes accessed | tf_op | source)
XLA Modules:
  0.0 372.8 jit_solution(3882063782726861215)
XLA Ops:
  1.9 5.1 %shard_map.169 = (bf16[960,128]{1,0:T(8,128)(2,1)S(1)}, bf16[960,128]{1,0:T(8,128)(2,1)S(1)}, bf16[240,1536]{1,0:T(8,128)(2,1)S(1)}, bf16[240,1536]{1,0:T(8,128)...) custom-call(s32[1]{0:T(128)} %bitcast.refs_0_, ...), custom_call_target="tpu_custom_call" | custom-call | tf_op jit(solution)/shard_map/pallas_call | solution.py:122
  8.7 7.9 %shard_map.170 = (bf16[240,1536]{1,0:T(8,128)(2,1)S(1)}, bf16[240,768]{1,0:T(8,128)(2,1)}, bf16[240,768]{1,0:T(8,128)(2,1)}, f32[240,8]{1,0:T(8,128)}, bf16[240,...) custom-call(s32[1]{0:T(128)} %bitcast.refs_0_, s32[4]{0:T(128)S(1)} %add_add_fusion.1.refs_1_, ...), custom_call_target="tpu_custom_call" | custom-call | tf_op jit(solution)/shard_map/pallas_call | solution.py:96
  19.6 9.6 %shard_map.171 = (bf16[240,1536]{1,0:T(8,128)(2,1)S(1)}, bf16[240,768]{1,0:T(8,128)(2,1)}, bf16[240,768]{1,0:T(8,128)(2,1)}, f32[240,8]{1,0:T(8,128)}, bf16[240,...) custom-call(s32[1]{0:T(128)} %bitcast.1.refs_0_, ...), custom_call_target="tpu_custom_call" | custom-call | tf_op jit(solution)/shard_map/pallas_call | solution.py:96
  33.1 3.7 collective-permute-done.2.refs_3_
  43.0 4.1 %shard_map.175 = (bf16[480,1152]{1,0:T(8,128)(2,1)S(1)}, bf16[480,1152]{1,0:T(8,128)(2,1)S(1)}, bf16[480,1152]{1,0:T(8,128)(2,1)S(1)}, bf16[480,1536]{1,0:T(8,128)(2,1)S(1)}, f32[8,128]{1,0:T(8,128)S(1)}) custom-call(bf16[128,1536]{1,0:T(8,128)(2,1)S(1)} %get-tuple-element.293.refs_0_, bf16[112,1536]{1,0:T(8,128)(2,1)S(1)} %get-tuple-element.294.refs_1_, ...), custom_call_target="tpu_custom_call" | custom-call | tf_op jit(solution)/shard_map/pallas_call | solution.py:122
  63.9 5.9 %shard_map.178 = (bf16[480,1152]{1,0:T(8,128)(2,1)S(1)}, bf16[480,1152]{1,0:T(8,128)(2,1)S(1)}, bf16[480,1152]{1,0:T(8,128)(2,1)S(1)}, bf16[480,1536]{1,0:T(8,128)(2,1)S(1)}, f32[8,128]{1,0:T(8,128)S(1)}) custom-call(bf16[128,1536]{1,0:T(8,128)(2,1)} %get-tuple-element.306.refs_0_, bf16[112,1536]{1,0:T(8,128)(2,1)} %get-tuple-element.307.refs_1_, ...), custom_call_target="tpu_custom_call" | custom-call | tf_op jit(solution)/shard_map/pallas_call | solution.py:122
  69.8 9.1 %shard_map.179 = (bf16[8,192,2304]{2,1,0:T(8,128)(2,1)S(1)}, f32[8,128]{1,0:T(8,128)S(1)}) custom-call(s32[2]{0:T(128)S(1)} %pad_add_fusion.refs_0_, bf16[480,1536]{1,0:T(8,128)(2,1)S(1)} %copy-done.37, bf16[480,1536]{1,0:T(8,128)(2,1)S(1)} %get-tuple-element.313.refs_2_, bf16[480,1152]{1,0:T(8,128)(2,1)S(1)} %copy-done.21, ...), custom_call_target="tpu_custom_call" | custom-call | tf_op jit(solution)/shard_map/pallas_call | solution.py:122
  83.8 4.5 %shard_map.181 = (bf16[8,144,1536]{2,1,0:T(8,128)(2,1)S(1)}, f32[8,128]{1,0:T(8,128)S(1)}) custom-call(s32[2]{0:T(128)S(1)} %pad_add_fusion.refs_0_, bf16[480,1152]{1,0:T(8,128)(2,1)S(1)} %copy-done.18, bf16[480,1152]{1,0:T(8,128)(2,1)S(1)} %get-tuple-element.310.refs_2_.refs_0_, bf16[480,1536]{1,0:T(8,128)(2,1)S(1)} %copy-done.14, ...), custom_call_target="tpu_custom_call" | custom-call | tf_op jit(solution)/shard_map/pallas_call | solution.py:122
  92.7 4.5 %collective-permute-done.9 = bf16[144,1536]{1,0:T(8,128)(2,1)S(1)} collective-permute-done((bf16[144,1536]{1,0:T(8,128)(2,1)S(1)}, bf16[144,1536]{1,0:T(8,128)(2,1)S(1)}, u32[]{:S(2)}, u32[]{:S(2)}) %collective-permute-start.9) | collective-permute-done | bytes 442400 | tf_op jit(solution)/shard_map/ppermute | solution.py:513
  110.2 5.0 %collective-permute-done.13 = bf16[192,2304]{1,0:T(8,128)(2,1)S(1)} collective-permute-done((bf16[192,2304]{1,0:T(8,128)(2,1)S(1)}, bf16[192,2304]{1,0:T(8,128)(2,1)S(1)}, u32[]{:S(2)}, u32[]{:S(2)}) %collective-permute-start.13) | collective-permute-done | bytes 884768 | tf_op jit(solution)/shard_map/ppermute | solution.py:513
  115.4 4.5 %collective-permute-done.12 = bf16[144,1536]{1,0:T(8,128)(2,1)S(1)} collective-permute-done((bf16[144,1536]{1,0:T(8,128)(2,1)S(1)}, bf16[144,1536]{1,0:T(8,128)(2,1)S(1)}, u32[]{:S(2)}, u32[]{:S(2)}) %collective-permute-start.12) | collective-permute-done | bytes 442400 | tf_op jit(solution)/shard_map/ppermute | solution.py:513
  130.7 3.5 shard_map.185
  134.2 5.8 %collective-permute-done.19.refs_2_ = bf16[240,1536]{1,0:T(8,128)(2,1)S(1)} collective-permute-done((bf16[240,1536]{1,0:T(8,128)(2,1)S(1)}, bf16[240,1536]{1,0:T(8,128)(2,1)S(1)}, u32[]{:S(2)}, u32[]{:S(2)}) %collective-permute-start.19) | collective-permute-done | bytes 737312 | tf_op jit(solution)/shard_map/ppermute | solution.py:67
  146.5 5.9 %shard_map.187 = (bf16[240,768]{1,0:T(8,128)(2,1)S(1)}, f32[480,256]{1,0:T(8,128)S(1)}, bf16[480,256]{1,0:T(8,128)(2,1)S(1)}, f32[8,128]{1,0:T(8,128)S(1)}) custom-call(s32[1]{0:T(128)} %bitcast.refs_0_, bf16[240,768]{1,0:T(8,128)(2,1)S(1)} %copy-done.67, f32[240,8]{1,0:T(8,128)S(1)} %copy-done.79, bf16[240,768]{1,0:T(8,128)(2,1)S(1)} %get-tuple-element.368.refs_3_, ...), custom_call_target="tpu_custom_call" | custom-call | tf_op jit(solution)/shard_map/pallas_call | solution.py:96
  154.2 3.7 shard_map.188
  157.9 3.3 collective-permute-done.23
  170.8 4.6 %collective-permute-done.27 = bf16[192,2304]{1,0:T(8,128)(2,1)S(1)} collective-permute-done((bf16[192,2304]{1,0:T(8,128)(2,1)S(1)}, bf16[192,2304]{1,0:T(8,128)(2,1)S(1)}, u32[]{:S(2)}, u32[]{:S(2)}) %collective-permute-start.27) | collective-permute-done | bytes 884768 | tf_op jit(solution)/shard_map/ppermute | solution.py:513
  178.8 4.7 %collective-permute-done.26 = bf16[480,256]{1,0:T(8,128)(2,1)S(1)} collective-permute-done((bf16[480,256]{1,0:T(8,128)(2,1)S(1)}, bf16[480,256]{1,0:T(8,128)(2,1)S(1)}, u32[]{:S(2)}, u32[]{:S(2)}) %collective-permute-start.26) | collective-permute-done | bytes 245792 | tf_op jit(solution)/shard_map/ppermute | solution.py:67
  213.8 3.2 collective-permute-done.33
  231.8 3.9 %shard_map.195 = (f32[8,144,1536]{2,1,0:T(8,128)}, f32[8,128]{1,0:T(8,128)S(1)}) custom-call(s32[2]{0:T(128)S(1)} %copy-done.82, bf16[144,1536]{1,0:T(8,128)(2,1)S(1)} %copy-done.35, bf16[144,1536]{1,0:T(8,128)(2,1)S(1)} %copy-done.64, bf16[144,1536]{1,0:T(8,128)(2,1)S(1)} %collective-permute-done.34.refs_3_, ...), custom_call_target="tpu_custom_call" | custom-call | tf_op jit(solution)/shard_map/pallas_call | solution.py:96
  246.0 3.3 shard_map.196
  253.8 7.8 %collective-permute-done.40.refs_3_ = bf16[192,2304]{1,0:T(8,128)(2,1)} collective-permute-done((bf16[192,2304]{1,0:T(8,128)(2,1)}, bf16[192,2304]{1,0:T(8,128)(2,1)}, u32[]{:S(2)}, u32[]{:S(2)}) %collective-permute-start.40) | collective-permute-done | bytes 884768 | tf_op jit(solution)/shard_map/ppermute | solution.py:513
  273.1 3.7 collective-permute-done.48
  284.8 7.1 %collective-permute-done.55 = bf16[792,128]{1,0:T(8,128)(2,1)S(1)} collective-permute-done((bf16[792,128]{1,0:T(8,128)(2,1)S(1)}, bf16[792,128]{1,0:T(8,128)(2,1)S(1)}, u32[]{:S(2)}, u32[]{:S(2)}) %collective-permute-start.55) | collective-permute-done | bytes 202784 | tf_op jit(solution)/shard_map/ppermute | solution.py:560
  292.8 5.3 %shard_map.198 = (f32[2,8,192,1152]{3,2,1,0:T(8,128)}, f32[8,128]{1,0:T(8,128)S(1)}) custom-call(s32[2]{0:T(128)S(1)} %copy-done.82, bf16[192,2304]{1,0:T(8,128)(2,1)S(1)} %copy-done.33, bf16[192,2304]{1,0:T(8,128)(2,1)} %collective-permute-done.37.refs_2_, bf16[192,2304]{1,0:T(8,128)(2,1)} %collective-permute-done.40.refs_3_, ...), custom_call_target="tpu_custom_call" | custom-call | tf_op jit(solution)/shard_map/pallas_call | solution.py:96
  300.3 4.2 %collective-permute-start.54 = (bf16[192,768]{1,0:T(8,128)(2,1)S(1)}, bf16[192,768]{1,0:T(8,128)(2,1)S(1)}, u32[]{:S(2)}, u32[]{:S(2)}) collective-permute-start(bf16[192,768]{1,0:T(8,128)(2,1)S(1)} %collective-permute-done.53.refs_3_), channel_id=1, source_target_pairs={{0,8},{8,16},{16,24},{24,28},{28,20},{20,12},{12,4},{4,0},{5,13},{... | collective-permute-start | bytes 884744 | tf_op jit(solution)/shard_map/ppermute | solution.py:513
  324.0 4.0 %shard_map.199 = (bf16[960,1536]{1,0:T(8,128)(2,1)}, bf16[960,1536]{1,0:T(8,128)(2,1)}, f32[8,128]{1,0:T(8,128)S(1)}) custom-call(s32[4]{0:T(128)S(1)} %add_add_fusion.refs_0_, bf16[240,1536]{1,0:T(8,128)(2,1)S(1)} %add_convert_fusion.2.refs_1_, bf16[240,1536]{1,0:T(8,128)(2,1)S(1)} %add_convert_fusion.1.refs_2_, ...), custom_call_target="tpu_custom_call" | custom-call | tf_op jit(solution)/shard_map/pallas_call | solution.py:122
  328.0 3.5 collective-permute-done.65.refs_3_
  344.0 3.9 %shard_map.200 = (f32[8,144,1536]{2,1,0:T(8,128)}, f32[8,128]{1,0:T(8,128)S(1)}) custom-call(s32[2]{0:T(128)S(1)} %copy-done.82, bf16[144,1536]{1,0:T(8,128)(2,1)} %collective-permute-done.41.refs_1_, bf16[144,1536]{1,0:T(8,128)(2,1)S(1)} %copy-done.66, bf16[144,1536]{1,0:T(8,128)(2,1)S(1)} %collective-permute-done.65.refs_3_, ...), custom_call_target="tpu_custom_call", output_to_operand_aliasing={{0}: (5, {})} | custom-call | tf_op jit(solution)/shard_map/pallas_call | solution.py:96
  348.0 4.3 %collective-permute-done.68.refs_1_ = bf16[192,768]{1,0:T(8,128)(2,1)S(1)} collective-permute-done((bf16[192,768]{1,0:T(8,128)(2,1)S(1)}, bf16[192,768]{1,0:T(8,128)(2,1)S(1)}, u32[]{:S(2)}, u32[]{:S(2)}) %collective-permute-start.68) | collective-permute-done | bytes 294944 | tf_op jit(solution)/shard_map/ppermute | solution.py:513
  358.3 4.8 %shard_map.201 = (f32[2,8,192,1152]{3,2,1,0:T(8,128)}, f32[8,128]{1,0:T(8,128)S(1)}) custom-call(s32[2]{0:T(128)S(1)} %copy-done.82, bf16[192,2304]{1,0:T(8,128)(2,1)} %collective-permute-done.63.refs_1_, bf16[192,2304]{1,0:T(8,128)(2,1)} %collective-permute-done.67.refs_2_, ...), custom_call_target="tpu_custom_call", output_to_operand_aliasing={{0}: (4, {})} | custom-call | tf_op jit(solution)/shard_map/pallas_call | solution.py:96
  363.1 3.4 shard_map.202
  (404 shorter events, 212.6 us)
Async XLA Ops:
  16.6 20.2 %collective-permute-start.2 = (bf16[240,1536]{1,0:T(8,128)(2,1)S(1)}, bf16[240,1536]{1,0:T(8,128)(2,1)S(1)}, u32[]{:S(2)}, u32[]{:S(2)}) collective-permute-start(bf16[240,1536]{1,0:T(8,128)(2,1)S(1)} %get-tuple-element.284.refs_2_), channel_id=1, source_target_pairs={{0,2},{1,3},{2,0},{3,1},{4,6},{5,7},{6,4},{7,5},{8,10},{9,11},{10,... | collective-permute-start | bytes 2211848 | tf_op jit(solution)/shard_map/ppermute | solution.py:67
  29.2 23.2 %collective-permute-start.5 = (bf16[240,1536]{1,0:T(8,128)(2,1)S(1)}, bf16[240,1536]{1,0:T(8,128)(2,1)S(1)}, u32[]{:S(2)}, u32[]{:S(2)}) collective-permute-start(bf16[240,1536]{1,0:T(8,128)(2,1)S(1)} %get-tuple-element.301.refs_2_), channel_id=1, source_target_pairs={{0,2},{1,3},{2,0},{3,1},{4,6},{5,7},{6,4},{7,5},{8,10},{9,11},{10,... | collective-permute-start | bytes 2211848 | tf_op jit(solution)/shard_map/ppermute | solution.py:67
  56.9 24.6 %collective-permute-start.8 = (bf16[240,1536]{1,0:T(8,128)(2,1)}, bf16[240,1536]{1,0:T(8,128)(2,1)S(1)}, u32[]{:S(2)}, u32[]{:S(2)}) collective-permute-start(bf16[240,1536]{1,0:T(8,128)(2,1)} %copy-done.90), channel_id=1, source_target_pairs={{0,1},{1,0},{2,3},{3,2},{4,5},{5,4},{6,7},{7,6},{8,9},{9,8},{10,11... | collective-permute-start | bytes 2211848 | tf_op jit(solution)/shard_map/ppermute | solution.py:63
  99.5 15.7 %collective-permute-start.13 = (bf16[192,2304]{1,0:T(8,128)(2,1)S(1)}, bf16[192,2304]{1,0:T(8,128)(2,1)S(1)}, u32[]{:S(2)}, u32[]{:S(2)}) collective-permute-start(bf16[192,2304]{1,0:T(8,128)(2,1)S(1)} %fusion.6), channel_id=1, source_target_pairs={{0,8},{8,16},{16,24},{24,28},{28,20},{20,12},{12,4},{4,0},{5,13},{... | collective-permute-start | bytes 2654216 | tf_op jit(solution)/shard_map/ppermute | solution.py:513
  103.4 21.9 %collective-permute-start.16 = (bf16[240,1536]{1,0:T(8,128)(2,1)S(1)}, bf16[240,1536]{1,0:T(8,128)(2,1)S(1)}, u32[]{:S(2)}, u32[]{:S(2)}) collective-permute-start(bf16[240,1536]{1,0:T(8,128)(2,1)S(1)} %get-tuple-element.343.refs_1_), channel_id=1, source_target_pairs={{0,2},{1,3},{2,0},{3,1},{4,6},{5,7},{6,4},{7,5},{8,10},{9,11},{10,... | collective-permute-start | bytes 2211848 | tf_op jit(solution)/shard_map/ppermute | solution.py:67
  105.8 14.1 %collective-permute-start.12 = (bf16[144,1536]{1,0:T(8,128)(2,1)S(1)}, bf16[144,1536]{1,0:T(8,128)(2,1)S(1)}, u32[]{:S(2)}, u32[]{:S(2)}) collective-permute-start(bf16[144,1536]{1,0:T(8,128)(2,1)S(1)} %fusion.16), channel_id=1, source_target_pairs={{0,8},{8,16},{16,24},{24,28},{28,20},{20,12},{12,4},{4,0},{5,13},{... | collective-permute-start | bytes 1327112 | tf_op jit(solution)/shard_map/ppermute | solution.py:513
  122.2 20.8 %collective-permute-start.18 = (bf16[192,2304]{1,0:T(8,128)(2,1)S(1)}, bf16[192,2304]{1,0:T(8,128)(2,1)S(1)}, u32[]{:S(2)}, u32[]{:S(2)}) collective-permute-start(bf16[192,2304]{1,0:T(8,128)(2,1)S(1)} %fusion.5), channel_id=1, source_target_pairs={{0,8},{8,16},{16,24},{24,28},{28,20},{20,12},{12,4},{4,0},{5,13},{... | collective-permute-start | bytes 2654216 | tf_op jit(solution)/shard_map/ppermute | solution.py:513
  123.8 16.2 %collective-permute-start.19 = (bf16[240,1536]{1,0:T(8,128)(2,1)S(1)}, bf16[240,1536]{1,0:T(8,128)(2,1)S(1)}, u32[]{:S(2)}, u32[]{:S(2)}) collective-permute-start(bf16[240,1536]{1,0:T(8,128)(2,1)S(1)} %get-tuple-element.351.refs_1_), channel_id=1, source_target_pairs={{0,2},{1,3},{2,0},{3,1},{4,6},{5,7},{6,4},{7,5},{8,10},{9,11},{10,... | collective-permute-start | bytes 2211848 | tf_op jit(solution)/shard_map/ppermute | solution.py:67
  128.5 14.8 %collective-permute-start.17 = (bf16[144,1536]{1,0:T(8,128)(2,1)S(1)}, bf16[144,1536]{1,0:T(8,128)(2,1)S(1)}, u32[]{:S(2)}, u32[]{:S(2)}) collective-permute-start(bf16[144,1536]{1,0:T(8,128)(2,1)S(1)} %fusion.14), channel_id=1, source_target_pairs={{0,8},{8,16},{16,24},{24,28},{28,20},{20,12},{12,4},{4,0},{5,13},{... | collective-permute-start | bytes 1327112 | tf_op jit(solution)/shard_map/ppermute | solution.py:513
  144.9 16.3 %collective-permute-start.23 = (bf16[192,2304]{1,0:T(8,128)(2,1)S(1)}, bf16[192,2304]{1,0:T(8,128)(2,1)S(1)}, u32[]{:S(2)}, u32[]{:S(2)}) collective-permute-start(bf16[192,2304]{1,0:T(8,128)(2,1)S(1)} %fusion.4), channel_id=1, source_target_pairs={{0,8},{8,16},{16,24},{24,28},{28,20},{20,12},{12,4},{4,0},{5,13},{... | collective-permute-start | bytes 2654216 | tf_op jit(solution)/shard_map/ppermute | solution.py:513
  157.9 28.7 %collective-permute-start.29 = (bf16[8,192,768]{2,1,0:T(8,128)(2,1)S(1)}, bf16[8,192,768]{2,1,0:T(8,128)(2,1)S(1)}, u32[]{:S(2)}, u32[]{:S(2)}) collective-permute-start(bf16[8,192,768]{2,1,0:T(8,128)(2,1)S(1)} %get-tuple-element.413), channel_id=1, source_target_pairs={{0,1},{1,0},{2,3},{3,2},{4,5},{5,4},{6,7},{7,6},{8,9},{9,8},{10,11... | collective-permute-start | bytes 7077896 | tf_op jit(solution)/shard_map/ppermute | solution.py:63
  169.3 14.9 %collective-permute-start.25 = (bf16[144,1536]{1,0:T(8,128)(2,1)S(1)}, bf16[144,1536]{1,0:T(8,128)(2,1)S(1)}, u32[]{:S(2)}, u32[]{:S(2)}) collective-permute-start(bf16[144,1536]{1,0:T(8,128)(2,1)S(1)} %fusion.11.refs_1_), channel_id=1, source_target_pairs={{0,8},{8,16},{16,24},{24,28},{28,20},{20,12},{12,4},{4,0},{5,13},{... | collective-permute-start | bytes 1327112 | tf_op jit(solution)/shard_map/ppermute | solution.py:513
  192.3 19.5 %collective-permute-start.35 = (bf16[192,2304]{1,0:T(8,128)(2,1)}, bf16[192,2304]{1,0:T(8,128)(2,1)}, u32[]{:S(2)}, u32[]{:S(2)}) collective-permute-start(bf16[192,2304]{1,0:T(8,128)(2,1)} %fusion.1), channel_id=1, source_target_pairs={{0,8},{8,16},{16,24},{24,28},{28,20},{20,12},{12,4},{4,0},{5,13},{... | collective-permute-start | bytes 2654216 | tf_op jit(solution)/shard_map/ppermute | solution.py:513
  198.7 26.5 %collective-permute-start.24 = (bf16[240,1536]{1,0:T(8,128)(2,1)}, bf16[240,1536]{1,0:T(8,128)(2,1)S(1)}, u32[]{:S(2)}, u32[]{:S(2)}) collective-permute-start(bf16[240,1536]{1,0:T(8,128)(2,1)} %copy-done.89), channel_id=1, source_target_pairs={{0,1},{1,0},{2,3},{3,2},{4,5},{5,4},{6,7},{7,6},{8,9},{9,8},{10,11... | collective-permute-start | bytes 2211848 | tf_op jit(solution)/shard_map/ppermute | solution.py:63
  198.7 15.1 %collective-permute-start.34 = (bf16[144,1536]{1,0:T(8,128)(2,1)}, bf16[144,1536]{1,0:T(8,128)(2,1)S(1)}, u32[]{:S(2)}, u32[]{:S(2)}) collective-permute-start(bf16[144,1536]{1,0:T(8,128)(2,1)} %copy-done.63), channel_id=1, source_target_pairs={{0,8},{8,16},{16,24},{24,28},{28,20},{20,12},{12,4},{4,0},{5,13},{... | collective-permute-start | bytes 1327112 | tf_op jit(solution)/shard_map/ppermute | solution.py:513
  200.5 20.5 %collective-permute-start.28 = (bf16[240,1536]{1,0:T(8,128)(2,1)}, bf16[240,1536]{1,0:T(8,128)(2,1)S(1)}, u32[]{:S(2)}, u32[]{:S(2)}) collective-permute-start(bf16[240,1536]{1,0:T(8,128)(2,1)} %copy-done.57), channel_id=1, source_target_pairs={{0,2},{1,3},{2,0},{3,1},{4,6},{5,7},{6,4},{7,5},{8,10},{9,11},{10,... | collective-permute-start | bytes 2211848 | tf_op jit(solution)/shard_map/ppermute | solution.py:67
  219.5 26.5 %collective-permute-start.45 = (bf16[240,1536]{1,0:T(8,128)(2,1)S(1)}, bf16[240,1536]{1,0:T(8,128)(2,1)S(1)}, u32[]{:S(2)}, u32[]{:S(2)}) collective-permute-start(bf16[240,1536]{1,0:T(8,128)(2,1)S(1)} %get-tuple-element.457.refs_2_), channel_id=1, source_target_pairs={{0,2},{1,3},{2,0},{3,1},{4,6},{5,7},{6,4},{7,5},{8,10},{9,11},{10,... | collective-permute-start | bytes 2211848 | tf_op jit(solution)/shard_map/ppermute | solution.py:67
  230.6 40.3 %collective-permute-start.51 = (bf16[240,1536]{1,0:T(8,128)(2,1)}, bf16[240,1536]{1,0:T(8,128)(2,1)}, u32[]{:S(2)}, u32[]{:S(2)}) collective-permute-start(bf16[240,1536]{1,0:T(8,128)(2,1)} %get-tuple-element.479), channel_id=1, source_target_pairs={{0,1},{1,0},{2,3},{3,2},{4,5},{5,4},{6,7},{7,6},{8,9},{9,8},{10,11... | collective-permute-start | bytes 2211848 | tf_op jit(solution)/shard_map/ppermute | solution.py:63
  231.4 22.5 %collective-permute-start.41 = (bf16[144,1536]{1,0:T(8,128)(2,1)}, bf16[144,1536]{1,0:T(8,128)(2,1)}, u32[]{:S(2)}, u32[]{:S(2)}) collective-permute-start(bf16[144,1536]{1,0:T(8,128)(2,1)} %collective-permute-done.38.refs_4_), channel_id=1, source_target_pairs={{0,8},{8,16},{16,24},{24,28},{28,20},{20,12},{12,4},{4,0},{5,13},{... | collective-permute-start | bytes 1327112 | tf_op jit(solution)/shard_map/ppermute | solution.py:513
  244.4 17.2 %collective-permute-start.40 = (bf16[192,2304]{1,0:T(8,128)(2,1)}, bf16[192,2304]{1,0:T(8,128)(2,1)}, u32[]{:S(2)}, u32[]{:S(2)}) collective-permute-start(bf16[192,2304]{1,0:T(8,128)(2,1)} %collective-permute-done.37.refs_2_), channel_id=1, source_target_pairs={{0,8},{8,16},{16,24},{24,28},{28,20},{20,12},{12,4},{4,0},{5,13},{... | collective-permute-start | bytes 2654216 | tf_op jit(solution)/shard_map/ppermute | solution.py:513
  252.7 14.2 %collective-permute-start.49 = (bf16[192,768]{1,0:T(8,128)(2,1)S(1)}, bf16[192,768]{1,0:T(8,128)(2,1)S(1)}, u32[]{:S(2)}, u32[]{:S(2)}) collective-permute-start(bf16[192,768]{1,0:T(8,128)(2,1)S(1)} %fusion.19), channel_id=1, source_target_pairs={{0,8},{8,16},{16,24},{24,28},{28,20},{20,12},{12,4},{4,0},{5,13},{... | collective-permute-start | bytes 884744 | tf_op jit(solution)/shard_map/ppermute | solution.py:513
  261.6 20.7 %collective-permute-start.46 = (bf16[192,2304]{1,0:T(8,128)(2,1)}, bf16[192,2304]{1,0:T(8,128)(2,1)S(1)}, u32[]{:S(2)}, u32[]{:S(2)}) collective-permute-start(bf16[192,2304]{1,0:T(8,128)(2,1)} %collective-permute-done.40.refs_3_), channel_id=1, source_target_pairs={{0,8},{8,16},{16,24},{24,28},{28,20},{20,12},{12,4},{4,0},{5,13},{... | collective-permute-start | bytes 2654216 | tf_op jit(solution)/shard_map/ppermute | solution.py:513
  270.0 22.7 %collective-permute-start.36 = (bf16[240,1536]{1,0:T(8,128)(2,1)S(1)}, bf16[240,1536]{1,0:T(8,128)(2,1)S(1)}, u32[]{:S(2)}, u32[]{:S(2)}) collective-permute-start(bf16[240,1536]{1,0:T(8,128)(2,1)S(1)} %copy-done.49), channel_id=1, source_target_pairs={{0,2},{1,3},{2,0},{3,1},{4,6},{5,7},{6,4},{7,5},{8,10},{9,11},{10,... | collective-permute-start | bytes 2211848 | tf_op jit(solution)/shard_map/ppermute | solution.py:67
  282.3 30.5 %collective-permute-start.63 = (bf16[192,2304]{1,0:T(8,128)(2,1)S(1)}, bf16[192,2304]{1,0:T(8,128)(2,1)}, u32[]{:S(2)}, u32[]{:S(2)}) collective-permute-start(bf16[192,2304]{1,0:T(8,128)(2,1)S(1)} %collective-permute-done.46.refs_4_), channel_id=1, source_target_pairs={{0,8},{8,16},{16,24},{24,28},{28,20},{20,12},{12,4},{4,0},{5,13},{... | collective-permute-start | bytes 2654216 | tf_op jit(solution)/shard_map/ppermute | solution.py:513
  284.8 15.5 %collective-permute-start.53 = (bf16[192,768]{1,0:T(8,128)(2,1)S(1)}, bf16[192,768]{1,0:T(8,128)(2,1)S(1)}, u32[]{:S(2)}, u32[]{:S(2)}) collective-permute-start(bf16[192,768]{1,0:T(8,128)(2,1)S(1)} %collective-permute-done.50.refs_2_), channel_id=1, source_target_pairs={{0,8},{8,16},{16,24},{24,28},{28,20},{20,12},{12,4},{4,0},{5,13},{... | collective-permute-start | bytes 884744 | tf_op jit(solution)/shard_map/ppermute | solution.py:513
  284.8 30.4 %collective-permute-start.60 = (bf16[240,1536]{1,0:T(8,128)(2,1)S(1)}, bf16[240,1536]{1,0:T(8,128)(2,1)S(1)}, u32[]{:S(2)}, u32[]{:S(2)}) collective-permute-start(bf16[240,1536]{1,0:T(8,128)(2,1)S(1)} %copy-done.55), channel_id=1, source_target_pairs={{0,1},{1,0},{2,3},{3,2},{4,5},{5,4},{6,7},{7,6},{8,9},{9,8},{10,11... | collective-permute-start | bytes 2211848 | tf_op jit(solution)/shard_map/ppermute | solution.py:63
  292.0 18.4 %collective-permute-start.52 = (bf16[240,1536]{1,0:T(8,128)(2,1)S(1)}, bf16[240,1536]{1,0:T(8,128)(2,1)S(1)}, u32[]{:S(2)}, u32[]{:S(2)}) collective-permute-start(bf16[240,1536]{1,0:T(8,128)(2,1)S(1)} %get-tuple-element.499), channel_id=1, source_target_pairs={{0,2},{1,3},{2,0},{3,1},{4,6},{5,7},{6,4},{7,5},{8,10},{9,11},{10,... | collective-permute-start | bytes 2211848 | tf_op jit(solution)/shard_map/ppermute | solution.py:67
  305.1 15.7 %collective-permute-start.59 = (bf16[240,1536]{1,0:T(8,128)(2,1)}, bf16[240,1536]{1,0:T(8,128)(2,1)}, u32[]{:S(2)}, u32[]{:S(2)}) collective-permute-start(bf16[240,1536]{1,0:T(8,128)(2,1)} %get-tuple-element.501.refs_5_), channel_id=1, source_target_pairs={{0,1},{1,0},{2,3},{3,2},{4,5},{5,4},{6,7},{7,6},{8,9},{9,8},{10,11... | collective-permute-start | bytes 2211848 | tf_op jit(solution)/shard_map/ppermute | solution.py:63
  312.8 20.9 %collective-permute-start.67 = (bf16[192,2304]{1,0:T(8,128)(2,1)}, bf16[192,2304]{1,0:T(8,128)(2,1)}, u32[]{:S(2)}, u32[]{:S(2)}) collective-permute-start(bf16[192,2304]{1,0:T(8,128)(2,1)} %collective-permute-done.63.refs_1_), channel_id=1, source_target_pairs={{0,8},{8,16},{16,24},{24,28},{28,20},{20,12},{12,4},{4,0},{5,13},{... | collective-permute-start | bytes 2654216 | tf_op jit(solution)/shard_map/ppermute | solution.py:513
  320.8 18.9 %collective-permute-start.64 = (bf16[192,768]{1,0:T(8,128)(2,1)}, bf16[192,768]{1,0:T(8,128)(2,1)S(1)}, u32[]{:S(2)}, u32[]{:S(2)}) collective-permute-start(bf16[192,768]{1,0:T(8,128)(2,1)} %copy-done.77), channel_id=1, source_target_pairs={{0,8},{8,16},{16,24},{24,28},{28,20},{20,12},{12,4},{4,0},{5,13},{... | collective-permute-start | bytes 884744 | tf_op jit(solution)/shard_map/ppermute | solution.py:513
  333.8 18.6 %collective-permute-start.71 = (bf16[192,2304]{1,0:T(8,128)(2,1)}, bf16[192,2304]{1,0:T(8,128)(2,1)S(1)}, u32[]{:S(2)}, u32[]{:S(2)}) collective-permute-start(bf16[192,2304]{1,0:T(8,128)(2,1)} %collective-permute-done.67.refs_2_), channel_id=1, source_target_pairs={{0,8},{8,16},{16,24},{24,28},{28,20},{20,12},{12,4},{4,0},{5,13},{... | collective-permute-start | bytes 2654216 | tf_op jit(solution)/shard_map/ppermute | solution.py:513
  352.4 17.9 %collective-permute-start.72 = (bf16[192,2304]{1,0:T(8,128)(2,1)S(1)}, bf16[192,2304]{1,0:T(8,128)(2,1)S(1)}, u32[]{:S(2)}, u32[]{:S(2)}) collective-permute-start(bf16[192,2304]{1,0:T(8,128)(2,1)S(1)} %collective-permute-done.71.refs_3_), channel_id=1, source_target_pairs={{0,8},{8,16},{16,24},{24,28},{28,20},{20,12},{12,4},{4,0},{5,13},{... | collective-permute-start | bytes 2654216 | tf_op jit(solution)/shard_map/ppermute | solution.py:513
  (141 other events, 1296.8 us)
